TPU v7x, 32 devices: a whole 2x2x4 slice. The times are simulated.
32 devices in a mesh: view: 4 (over y, x), tm: 8 (over z, core).
Axes of the slice: x: 2, y: 2, z: 4, core: 2. Of those that a mesh axis runs over, the one named last changes fastest.
Arguments:
- frames: bfloat16 [4, 8192, 768], P('view', 'tm'), may hold values from -100 to 100
- conv_weight: bfloat16 [3, 768, 768], replicated, may hold values from -0.125 to 0.125
- conv_bias: float32 [768], replicated, may hold values from -4 to 4
- proj_weight: bfloat16 [768, 768], replicated, may hold values from -0.21875 to 0.21875
- frames_before: int32 [8192], P('tm'), may hold values from -1 to 1023, as said below
- frames_after: int32 [8192], P('tm'), may hold values from -1 to 1023, as said below
Outputs:
- whitened: float32 [4, 8192, 768], P('view', 'tm')
- pair_loss: float32 [4, 8192], P('view', 'tm')
Inputs may be any that keep to these rules, and one draw needn't show every extreme that they name: Live frames (frames_before >= 0) form clips of consecutive frames, each at most 1024 frames long; inside a clip frames_before counts up from 0 and frames_after counts down to 0; padding frames carry -1 in both lists, and the first and last frames of the timeline are live. `frames_after`: consistent with frames_before, as stated there.
All inputs are finite; a program needn't handle non-finite values.
Results may differ from a plain program's by a relative error of at most 0.0045.
Values may be sent and summed in bfloat16 or wider, within the bound.
A program may use at most 128 MiB of HBM per device.

v0:
```python
import jax
import jax.numpy as jnp
from jax import lax
from jax.sharding import PartitionSpec as P

DILATION_STEP = 4


eps_shrink = 0.001


def padded(shard, sides, width):
    for axis, dim in sides:
        count, length = (lax.axis_size(axis), shard.shape[dim])
        up = [(i, (i + 1) % count) for i in range(count - 1)]
        down = [(j, i) for i, j in up]
        last = lax.slice_in_dim(shard, length - width, length, axis=dim)
        first = lax.slice_in_dim(shard, 0, width, axis=dim)
        before = lax.ppermute(last, axis, up)
        after = lax.ppermute(first, axis, down)
        shard = jnp.concatenate([before, shard, after], axis=dim)
    return shard


def partner_2(value, axis, distance):
    mask = 2**distance
    pairs = [(source, source ^ mask) for source in range(lax.axis_size(axis))]
    return lax.ppermute(value, axis, pairs)


def per_device(frames, conv_weight, conv_bias, proj_weight, frames_before, frames_after):
    local_frames = frames[0]
    frame_rows = local_frames.shape[0]
    width = proj_weight.shape[1]
    live = (frames_before >= 0).astype(jnp.float32)
    padded_input = padded(local_frames, (("tm", 0),), DILATION_STEP)
    total = jnp.zeros((frame_rows, local_frames.shape[1]), jnp.float32)
    for frame_index in range(3):
        shift_amount = (frame_index - 1) * DILATION_STEP
        valid = ((frames_before >= -shift_amount) & (frames_after >= shift_amount)).astype(
            jnp.float32
        )
        shifted_input = padded_input[
            DILATION_STEP + shift_amount : DILATION_STEP + shift_amount + frame_rows
        ]
        term = jnp.dot(shifted_input, conv_weight[frame_index], preferred_element_type=jnp.float32)
        total = total + valid[:, None] * term
    hidden = (live[:, None] * jax.nn.gelu(total + conv_bias[None, :], approximate=True)).astype(
        jnp.bfloat16
    )
    embed = jnp.dot(hidden, proj_weight, preferred_element_type=jnp.float32)
    identity = jnp.eye(width, dtype=jnp.float32)
    count, sums = lax.psum((jnp.sum(live), jnp.sum(embed, axis=0)), "tm")
    mean = sums / count
    centered = live[:, None] * (embed - mean[None, :])
    gram = jnp.dot(
        centered.T, centered, precision=lax.Precision.HIGHEST, preferred_element_type=jnp.float32
    )
    cov = lax.psum(gram, "tm") / count + eps_shrink * identity
    factor = jnp.linalg.cholesky(cov)
    whitened = jax.scipy.linalg.solve_triangular(factor, centered.T, lower=True).T
    partner = partner_2(whitened, "view", 0)
    diff = whitened - partner
    pair_loss = jnp.sum(diff * diff, axis=1) / width
    return (whitened[None], pair_loss[None])


def solution(mesh):
    return jax.shard_map(
        per_device,
        mesh=mesh,
        in_specs=(P("view", "tm", None), P(), P(), P(), P("tm"), P("tm")),
        out_specs=(P("view", "tm", None), P("view", "tm")),
        check_vma=False,
    )
```

profile of v0, /device:TPU:0, one launch (start us, length us, event | category | flops | bytes accessed | tf_op | source)
XLA Modules:
  0.0 508.4 jit_solution(16603744037829397869)
XLA Ops:
  13.7 4.9 fusion.40
  18.6 4.4 fusion.21
  23.1 8.5 %fusion.92 = (f32[768]{0:T(1024)S(1)}, f32[1024,768]{1,0:T(8,128)}) fusion(bf16[768,768]{1,0:T(8,128)(2,1)S(1)} %copy-done, f32[1024,768]{1,0:T(8,128)} %fusion.40, f32[1024,768]{1,0:T(8,128)} %fusion.21, bf16[4,768]{1,0:T(4,128)(2,1)S(1)} %collective-permute-done.1, bf16[1024,768]{1,0:T(8,128)(2,1)S(1)} %bitcast.104, f32[768]{0:T(1024)S(1)} %copy-done.15, ...), kind=kOutput, calls=%fused_computation.161 | convolution fusion | flops 2432433408 | bytes 13398016 | tf_op jit(solution)/shard_map/dot_general | solution.py:51
  31.5 18.7 %all-reduce.1 = (f32[768]{0:T(1024)S(1)}, f32[]{:T(128)}) all-reduce(f32[768]{0:T(1024)S(1)} %get-tuple-element.56, f32[]{:T(128)} %get-tuple-element.26), channel_id=1, replica_groups=mesh['view'=4,'tm'=8] {'tm'}, use_global_device_ids=true, to_apply=%region_1.0 | all-reduce | flops 769 | bytes 6152 | tf_op jit(solution)/shard_map/psum | solution.py:53
  50.9 12.5 %fusion.10 = f32[768,768]{0,1:T(8,128)} fusion(f32[1024,768]{1,0:T(8,128)} %get-tuple-element.57, f32[768]{0:T(1024)S(1)} %broadcast_divide_fusion, f32[1024]{0:T(1024)S(1)} %get-tuple-element.55), kind=kOutput, calls=%fused_computation.15 | convolution fusion | flops 7249330176 | bytes 5512192 | tf_op jit(solution)/shard_map/dot_general | solution.py:56
  64.0 4.1 fusion.9
  68.1 60.5 %all-reduce.4.cloned.1.call-done = f32[768,768]{0,1:T(8,128)} async-done(((f32[768,768]{0,1:T(8,128)}), f32[768,768]{0,1:T(8,128)}) %all-reduce.4.cloned.1.call-update) | async-done | bytes 2359312 | tf_op jit(solution)/shard_map/psum | solution.py:59
  128.6 3.9 select_add_fusion
  139.9 11.7 %cholesky.164 = f32[128,128]{1,0:T(8,128)S(1)} custom-call(f32[128,128]{1,0:T(8,128)S(1)} %cholesky.421), custom_call_target="Cholesky" | custom-call | tf_op jit(solution)/shard_map/jit(cholesky)/cholesky | solution.py:60
  152.4 9.8 %custom-call.47 = f32[1,128,128]{1,2,0:T(8,128)S(1)} custom-call(f32[1,128,128]{2,1,0:T(8,128)S(1)} %get-tuple-element.51), custom_call_target="InvertDiagBlocksLowerTriangular" | custom-call | tf_op jit(solution)/shard_map/jit(cholesky)/cholesky | solution.py:60
  165.9 11.7 %cholesky.187 = f32[128,128]{1,0:T(8,128)S(1)} custom-call(f32[128,128]{1,0:T(8,128)S(1)} %cholesky.425), custom_call_target="Cholesky" | custom-call | tf_op jit(solution)/shard_map/jit(cholesky)/cholesky | solution.py:60
  178.4 10.8 %custom-call.48 = f32[1,128,128]{1,2,0:T(8,128)} custom-call(f32[1,128,128]{2,1,0:T(8,128)S(1)} %get-tuple-element.49), custom_call_target="InvertDiagBlocksLowerTriangular" | custom-call | tf_op jit(solution)/shard_map/jit(cholesky)/cholesky | solution.py:60
  194.1 13.2 %cholesky.352 = f32[128,128]{1,0:T(8,128)} custom-call(f32[128,128]{1,0:T(8,128)} %cholesky.430), custom_call_target="Cholesky" | custom-call | tf_op jit(solution)/shard_map/jit(cholesky)/cholesky | solution.py:60
  211.1 11.3 %custom-call.49 = f32[1,128,128]{1,2,0:T(8,128)} custom-call(f32[1,128,128]{2,1,0:T(8,128)} %get-tuple-element.47), custom_call_target="InvertDiagBlocksLowerTriangular" | custom-call | tf_op jit(solution)/shard_map/jit(cholesky)/cholesky | solution.py:60
  227.1 13.3 %cholesky.371 = f32[128,128]{1,0:T(8,128)} custom-call(f32[128,128]{1,0:T(8,128)} %cholesky.435), custom_call_target="Cholesky" | custom-call | tf_op jit(solution)/shard_map/jit(cholesky)/cholesky | solution.py:60
  244.3 11.3 %custom-call.50 = f32[1,128,128]{1,2,0:T(8,128)} custom-call(f32[1,128,128]{2,1,0:T(8,128)} %get-tuple-element.45), custom_call_target="InvertDiagBlocksLowerTriangular" | custom-call | tf_op jit(solution)/shard_map/jit(cholesky)/cholesky | solution.py:60
  259.9 13.2 %cholesky.390 = f32[128,128]{1,0:T(8,128)} custom-call(f32[128,128]{1,0:T(8,128)} %cholesky.440), custom_call_target="Cholesky" | custom-call | tf_op jit(solution)/shard_map/jit(cholesky)/cholesky | solution.py:60
  277.5 11.3 %custom-call.51 = f32[1,128,128]{1,2,0:T(8,128)} custom-call(f32[1,128,128]{2,1,0:T(8,128)} %get-tuple-element.43), custom_call_target="InvertDiagBlocksLowerTriangular" | custom-call | tf_op jit(solution)/shard_map/jit(cholesky)/cholesky | solution.py:60
  292.3 13.2 %cholesky.408 = f32[128,128]{1,0:T(8,128)} custom-call(f32[128,128]{1,0:T(8,128)} %convolution_subtract_fusion.7), custom_call_target="Cholesky" | custom-call | tf_op jit(solution)/shard_map/jit(cholesky)/cholesky | solution.py:60
  319.3 21.0 %while.1 = (s32[]{:T(128)}, f32[768,768]{0,1:T(8,128)}, s32[6,2]{0,1:T(2,128)S(1)}, f32[6,128,128]{2,1,0:T(8,128)}, s32[]{:T(128)}) while((s32[]{:T(128)}, f32[768,768]{0,1:T(8,128)}, s32[6,2]{0,1:T(2,128)S(1)}, f32[6,128,128]{2,1,0:T(8,128)}, s32[]{:T(128)}) %tuple.46), condition=%wide.while_cond, body=%wide.while_body.sunk | while | flops 2 | bytes 393329 | solution.py:61
  340.3 60.2 %custom-call.52 = f32[6,128,128]{1,2,0:T(8,128)S(1)} custom-call(f32[6,128,128]{2,1,0:T(8,128)} %get-tuple-element.9), custom_call_target="InvertDiagBlocksLowerTriangular" | custom-call | tf_op jit(solution)/shard_map/jit(_solve_triangular)/triangular_solve | solution.py:61
  416.2 4.4 fusion.34
  422.1 5.6 %convolution_subtract_fusion.1 = f32[128,1024]{0,1:T(8,128)S(1)} fusion(f32[640,1024]{1,0:T(8,128)S(1)} %get-tuple-element.32, f32[768,1024]{0,1:T(8,128)S(1)} %copy-done.1, f32[768,768]{0,1:T(8,128)} %get-tuple-element.110), kind=kOutput, calls=%fused_computation.47 | convolution fusion | flops 1006764032 | bytes 3997696 | tf_op jit(solution)/shard_map/jit(_solve_triangular)/triangular_solve | solution.py:61
  434.2 63.2 %collective-permute-done.2 = f32[1024,768]{0,1:T(8,128)} collective-permute-done((f32[1024,768]{0,1:T(8,128)}, f32[1024,768]{0,1:T(8,128)}, u32[]{:S(2)}, u32[]{:S(2)}) %collective-permute-start.2) | collective-permute-done | bytes 3145760 | tf_op jit(solution)/shard_map/ppermute | solution.py:28
  (133 shorter events, 108.5 us)
Async XLA Ops:
  7.2 15.9 %copy-start = (bf16[768,768]{1,0:T(8,128)(2,1)S(1)}, bf16[768,768]{1,0:T(8,128)(2,1)}, u32[]{:S(2)}) copy-start(bf16[768,768]{1,0:T(8,128)(2,1)} %param.9) | copy-start | bytes 3538948
  7.2 121.4 %all-reduce.4.cloned.1.call-start = ((), (), s32[]{:S(2)}) async-start(), calls=%async_computation | async-start | bytes 4718592 | tf_op jit(solution)/shard_map/psum | solution.py:59
  8.0 15.0 %collective-permute-start.1 = (bf16[4,768]{1,0:T(4,128)(2,1)S(1)}, bf16[4,768]{1,0:T(4,128)(2,1)S(1)}, u32[]{:S(2)}, u32[]{:S(2)}) collective-permute-start(bf16[4,768]{1,0:T(4,128)(2,1)S(1)} %get-tuple-element.30), channel_id=1, source_target_pairs={{1,0},{2,1},{3,2},{4,3},{5,4},{6,5},{7,6},{9,8},{10,9},{11,10},{12... | collective-permute-start | bytes 18440 | tf_op jit(solution)/shard_map/ppermute | solution.py:20
  9.3 9.3 %collective-permute-start = (bf16[4,768]{1,0:T(4,128)(2,1)S(1)}, bf16[4,768]{1,0:T(4,128)(2,1)S(1)}, u32[]{:S(2)}, u32[]{:S(2)}) collective-permute-start(bf16[4,768]{1,0:T(4,128)(2,1)S(1)} %get-tuple-element.31), channel_id=1, source_target_pairs={{0,1},{1,2},{2,3},{3,4},{4,5},{5,6},{6,7},{8,9},{9,10},{10,11},{11... | collective-permute-start | bytes 18440 | tf_op jit(solution)/shard_map/ppermute | solution.py:19
  13.7 4.9 copy-start.12
  13.7 4.9 copy-start.13
  13.7 4.9 copy-start.14
  18.6 4.4 copy-start.15
  132.5 3.4 copy-start.2
  138.5 1.4 copy-start.3
  165.0 13.4 %copy-start.4 = (f32[640,128]{1,0:T(8,128)}, f32[640,128]{1,0:T(8,128)S(1)}, u32[]{:S(2)}) copy-start(f32[640,128]{1,0:T(8,128)S(1)} %convolution_subtract_fusion.3) | copy-start | bytes 983044
  189.2 1.1 copy-start.6
  189.2 1.1 copy-start.10
  189.2 1.1 copy-start.5
  189.2 1.2 copy-start.11
  192.7 0.7 copy-start.7
  225.8 0.7 copy-start.8
  258.7 0.6 copy-start.9
  317.7 1.6 copy-start.16
  403.0 3.7 copy-start.1
  429.2 68.3 %collective-permute-start.2 = (f32[1024,768]{0,1:T(8,128)}, f32[1024,768]{0,1:T(8,128)}, u32[]{:S(2)}, u32[]{:S(2)}) collective-permute-start(f32[1024,768]{0,1:T(8,128)} %bitcast.24), channel_id=1, source_target_pairs={{0,8},{8,0},{16,24},{24,16},{1,9},{9,1},{17,25},{25,17},{2,10},{10... | collective-permute-start | bytes 9437192 | tf_op jit(solution)/shard_map/ppermute | solution.py:28
Sparse Core Ops, SparseCore 0:
  63.5 64.9 all-reduce.3
where the time goes:
time: 515 us; the launch traced here: 508 us
  other arithmetic  220 us (43%)
  waiting for transfers between devices  124 us (24%)
  matrix products  74.2 us (14%)
  local copies, waits for them, and re-layouts  47.1 us (9%)
  blocking collectives  18.7 us (4%)
  between operations  18.4 us (4%)
  starting transfers between devices  5.83 us (1%)
    another operation x22, other arithmetic, per_device(): factor = jnp.linalg.cholesky(cov)  142 us
    ppermute x1, waiting for transfers between devices, partner_2(): return lax.ppermute(value, axis, pairs)  63.2 us
    another operation x3, other arithmetic, per_device(): jax.scipy.linalg.solve_triangular(factor, centered.T, lower=True)  62.4 us
    psum x1, waiting for transfers between devices, per_device(): cov = lax.psum(gram, 'tm') / count + eps_shrink * identity  60.5 us
    another operation x11, matrix products, per_device(): jax.scipy.linalg.solve_triangular(factor, centered.T, lower=True)  28.6 us
    another operation x30, local copies, waits for them, and re-layouts  20.9 us
    psum x1, blocking collectives, per_device(): count, sums = lax.psum((jnp.sum(live), jnp.sum(embed, axis=0)), 'tm')  18.7 us
    another operation x10, matrix products, per_device(): factor = jnp.linalg.cholesky(cov)  15.2 us
  transfers between devices with their start and end apart: 4, of which 2 were waited for; matrix products, arithmetic and copies ran while one was open for 4% of the time, Pallas kernels for 0%

commit v1 on v0

v1 whole, which is shorter than its diff:
```python
import functools

import jax
import jax.numpy as jnp
from jax import lax
from jax.experimental import pallas as pl
from jax.experimental.pallas import tpu as pltpu
from jax.sharding import PartitionSpec as P

DILATION_STEP = 4
eps_shrink = 0.001
B = 128
R = 8
HIGHEST = lax.Precision.HIGHEST
NT = (((1,), (1,)), ((), ()))
NN = (((1,), (0,)), ((), ()))
TN = (((0,), (0,)), ((), ()))


def dot(a, b, dims, precision=HIGHEST):
    return lax.dot_general(a, b, dims, precision=precision, preferred_element_type=jnp.float32)


def split3(x):
    hi = x.astype(jnp.bfloat16).astype(jnp.float32)
    rest = x - hi
    mid = rest.astype(jnp.bfloat16).astype(jnp.float32)
    return hi, mid, rest - mid


def invert_factor(d_ref, w_ref):
    lane = lax.broadcasted_iota(jnp.int32, (R, B), 1)
    sub = lax.broadcasted_iota(jnp.int32, (R, B), 0)
    block_row = lax.broadcasted_iota(jnp.int32, (B, B), 0)
    block_lane = lax.broadcasted_iota(jnp.int32, (B, B), 1)

    def panel(p, carry):
        base = p * R
        rows = pl.ds(pl.multiple_of(base, R), R)
        part = d_ref[rows, :]
        front = pltpu.roll(part, lax.rem(B - base, B), 1)
        cols = [jnp.broadcast_to(front[:, j : j + 1], (R, B)) for j in range(R)]
        unit = jnp.where(lane == base + sub, 1.0, 0.0)
        scale = jnp.zeros((R, B), jnp.float32)
        for j in range(R):
            pivot = jnp.broadcast_to(cols[j][j : j + 1, :], (R, B))
            scale = jnp.where(sub == j, pivot, scale)
            if j + 1 < R:
                mult = jnp.where(sub > j, cols[j] * (1.0 / pivot), 0.0)
                for k in range(j + 1, R):
                    cols[k] = cols[k] - mult * jnp.broadcast_to(cols[k][j : j + 1, :], (R, B))
                part = part - mult * jnp.broadcast_to(part[j : j + 1, :], (R, B))
                unit = unit - mult * jnp.broadcast_to(unit[j : j + 1, :], (R, B))
        scale = lax.rsqrt(scale)
        upper = jnp.where(lane >= base + R, part * scale, 0.0)
        inverse = jnp.where(lane < base, part, unit) * scale
        w_ref[rows, :] = jnp.where(lane < base + R, inverse, 0.0)
        right = jnp.where(lane >= base + R, upper, inverse)
        ah, am, al = split3(upper)
        bh, bm, bl = split3(right)
        a = jnp.concatenate([ah, ah, am, am, ah, al], axis=0).astype(jnp.bfloat16)
        b = jnp.concatenate([bh, bm, bh, bm, bl, bh], axis=0).astype(jnp.bfloat16)
        keep = (block_row >= base + R) & (block_lane >= base) & (block_lane < base + R)
        d_ref[...] = jnp.where(keep, 0.0, d_ref[...]) - dot(a, b, TN, None)
        return carry

    lax.fori_loop(0, B // R, panel, 0)


def factor_kernel(n, gram_ref, inv_ref, d_ref, w_ref, m_ref):
    for i in range(n):
        at = B * (i * (i + 1) // 2)
        m_ref[pl.ds(i * B, B), pl.ds(0, (i + 1) * B)] = gram_ref[:, pl.ds(at, (i + 1) * B)]
    for k in range(n):
        rows = pl.ds(k * B, B)
        d_ref[...] = m_ref[rows, rows]
        invert_factor(d_ref, w_ref)
        w = w_ref[...]
        if k:
            inv_ref[rows, pl.ds(0, k * B)] = dot(w, m_ref[rows, pl.ds(0, k * B)], NN)
        inv_ref[rows, rows] = w
        if k + 1 < n:
            rest = (n - 1 - k) * B
            inv_ref[rows, pl.ds((k + 1) * B, rest)] = jnp.zeros((B, rest), jnp.float32)
            below = pl.ds((k + 1) * B, rest)
            panel = dot(m_ref[below, rows], w, NT)
            m_ref[below, rows] = -dot(panel, w, NN)
            if k:
                m_ref[below, pl.ds(0, k * B)] -= dot(panel, inv_ref[rows, pl.ds(0, k * B)], NN)
            for i in range(k + 1, n):
                a = panel[(i - k - 1) * B : (i - k) * B]
                m_ref[pl.ds(i * B, B), pl.ds((k + 1) * B, (i - k) * B)] -= dot(a, panel[: (i - k) * B], NT)


def inverse_factor(packed, width):
    n = width // B
    return pl.pallas_call(
        functools.partial(factor_kernel, n),
        out_shape=jax.ShapeDtypeStruct((width, width), jnp.float32),
        in_specs=[pl.BlockSpec(memory_space=pltpu.VMEM)],
        out_specs=pl.BlockSpec(memory_space=pltpu.VMEM),
        scratch_shapes=[
            pltpu.VMEM((B, B), jnp.float32),
            pltpu.VMEM((B, B), jnp.float32),
            pltpu.VMEM((width, width), jnp.float32),
        ],
        compiler_params=pltpu.CompilerParams(vmem_limit_bytes=32 * 1024 * 1024),
    )(packed)


def padded(shard, axis, width):
    count, length = (lax.axis_size(axis), shard.shape[0])
    up = [(i, (i + 1) % count) for i in range(count - 1)]
    down = [(j, i) for i, j in up]
    before = lax.ppermute(shard[length - width :], axis, up)
    after = lax.ppermute(shard[:width], axis, down)
    return jnp.concatenate([before, shard, after], axis=0)


def lower_blocks(rows_of, n):
    return jnp.concatenate([rows_of(i) for i in range(n)], axis=1)


def per_device(frames, conv_weight, conv_bias, proj_weight, frames_before, frames_after):
    local_frames = frames[0]
    frame_rows = local_frames.shape[0]
    width = proj_weight.shape[1]
    n = width // B
    live = (frames_before >= 0).astype(jnp.float32)
    padded_input = padded(local_frames, "tm", DILATION_STEP)
    total = jnp.zeros((frame_rows, local_frames.shape[1]), jnp.float32)
    for frame_index in range(3):
        shift_amount = (frame_index - 1) * DILATION_STEP
        valid = ((frames_before >= -shift_amount) & (frames_after >= shift_amount)).astype(
            jnp.float32
        )
        shifted_input = padded_input[
            DILATION_STEP + shift_amount : DILATION_STEP + shift_amount + frame_rows
        ]
        term = jnp.dot(shifted_input, conv_weight[frame_index], preferred_element_type=jnp.float32)
        total = total + valid[:, None] * term
    hidden = (live[:, None] * jax.nn.gelu(total + conv_bias[None, :], approximate=True)).astype(
        jnp.bfloat16
    )
    embed = jnp.dot(hidden, proj_weight, preferred_element_type=jnp.float32)

    local_count = jnp.sum(live)
    local_mean = jnp.sum(embed, axis=0) / jnp.maximum(local_count, 1.0)
    stats = lax.all_gather(
        jnp.concatenate([local_mean, jnp.broadcast_to(local_count, (B,))]), "tm"
    )
    about = live[:, None] * (embed - local_mean[None, :])
    gram = lower_blocks(
        lambda i: dot(about[:, i * B : (i + 1) * B], about[:, : (i + 1) * B], TN), n
    )
    gram = lax.psum(gram, "tm")
    counts = stats[:, width]
    means = stats[:, :width]
    count = jnp.sum(counts)
    mean = jnp.sum(counts[:, None] * means, axis=0) / count
    offset = jnp.sqrt(counts)[:, None] * (means - mean[None, :])
    between = lower_blocks(
        lambda i: dot(offset[:, i * B : (i + 1) * B], offset[:, : (i + 1) * B], TN), n
    )
    ridge = lower_blocks(lambda i: eps_shrink * jnp.eye(B, (i + 1) * B, i * B, dtype=jnp.float32), n)
    inverse = inverse_factor((gram + between) / count + ridge, width)
    centered = live[:, None] * (embed - mean[None, :])
    whitened = dot(centered, inverse, NT)

    half = frame_rows // 2
    bit = lax.axis_index("view") % 2
    pairs = [(i, i ^ 1) for i in range(lax.axis_size("view"))]
    sent = lax.dynamic_slice_in_dim(whitened, (1 - bit) * half, half).astype(jnp.bfloat16)
    partner = lax.ppermute(sent, "view", pairs).astype(jnp.float32)
    own = lax.dynamic_slice_in_dim(whitened, bit * half, half)
    diff = own - partner
    mine = jnp.sum(diff * diff, axis=1) / width
    theirs = lax.ppermute(mine, "view", pairs)
    pair_loss = jnp.where(bit == 0, jnp.concatenate([mine, theirs]), jnp.concatenate([theirs, mine]))
    return (whitened[None], pair_loss[None])


def solution(mesh):
    return jax.shard_map(
        per_device,
        mesh=mesh,
        in_specs=(P("view", "tm", None), P(), P(), P(), P("tm"), P("tm")),
        out_specs=(P("view", "tm", None), P("view", "tm")),
        check_vma=False,
    )
```

time: 515 us -> 228 us (0.44); the launches traced: 508 us -> 228 us
  other arithmetic: 220 us -> 10.5 us
  Pallas kernels: 0 us -> 50.8 us
  waiting for transfers between devices: 124 us -> 74.2 us
  local copies, waits for them, and re-layouts: 47.1 us -> 6.82 us
  matrix products: 74.2 us -> 46.2 us
    another operation x25 -> x0, other arithmetic: 204 us -> none  [the longest x22 142 us: per_device(): factor = jnp.linalg.cholesky(cov)]
    pallas_call x0 -> x1, Pallas kernels: none -> 50.8 us  [inverse_factor(): pl.pallas_call(functools.partial(factor_kernel, n), out_shape=jax.ShapeDt...]
    ppermute x3 -> x4, waiting for transfers between devices: 63.2 us -> 16.3 us  [the longest x1 16.3 us: per_device(): partner = lax.ppermute(sent, 'view', pairs).astype(jnp.float32)]
    another operation x21 -> x0, matrix products: 43.8 us -> none  [the longest x11 28.6 us: per_device(): jax.scipy.linalg.solve_triangular(factor, centered.T, lower=True)]
    another operation x50 -> x0, local copies, waits for them, and re-layouts: 35.8 us -> none
    psum x1 -> x0, blocking collectives: 18.7 us -> none  [per_device(): count, sums = lax.psum((jnp.sum(live), jnp.sum(embed, axis=0)), 'tm')]
    all_gather x0 -> x1, blocking collectives: none -> 17.7 us  [per_device(): lax.all_gather(jnp.concatenate([local_mean, jnp.broadcast_to(local_count,...]
    dot_general x1 -> x13, matrix products: 12.5 us -> 27.6 us  [dot(): lax.dot_general(a, b, dims, precision=precision, preferred_element_type=j...]
  transfers between devices with their start and end apart: 4 -> 5, of which waited for: 2 -> 2; matrix products, arithmetic and copies ran while one was open for 4% -> 8% of each run, Pallas kernels for 0% -> 0%
where the time goes in v1:
time: 228 us
  waiting for transfers between devices  74.2 us (33%)
  Pallas kernels  50.8 us (22%)
  matrix products  46.2 us (20%)
  blocking collectives  17.7 us (8%)
  between operations  14.9 us (7%)
  other arithmetic  10.5 us (5%)
  local copies, waits for them, and re-layouts  6.82 us (3%)
  starting transfers between devices  6.67 us (3%)
    psum x1, waiting for transfers between devices, per_device(): gram = lax.psum(gram, 'tm')  57.9 us
    pallas_call x1, Pallas kernels, inverse_factor(): pl.pallas_call(functools.partial(factor_kernel, n), out_shape=jax.ShapeDt...  50.8 us
    dot_general x13, matrix products, dot(): lax.dot_general(a, b, dims, precision=precision, preferred_element_type=j...  27.6 us
    all_gather x1, blocking collectives, per_device(): lax.all_gather(jnp.concatenate([local_mean, jnp.broadcast_to(local_count,...  17.7 us
    ppermute x1, waiting for transfers between devices, per_device(): partner = lax.ppermute(sent, 'view', pairs).astype(jnp.float32)  16.3 us
    dot_general x2, matrix products, per_device(): jnp.dot(shifted_input, conv_weight[frame_index], preferred_element_type=j...  9.69 us
    dot_general x1, matrix products, per_device(): embed = jnp.dot(hidden, proj_weight, preferred_element_type=jnp.float32)  8.93 us
    unnamed x15, local copies, waits for them, and re-layouts  5.23 us
  transfers between devices with their start and end apart: 5, of which 2 were waited for; matrix products, arithmetic and copies ran while one was open for 8% of the time, Pallas kernels for 0%

profile of v1, /device:TPU:0, one launch (start us, length us, event | category | flops | bytes accessed | tf_op | source)
XLA Modules:
  0.0 227.8 jit_solution(3139797334803513858)
XLA Ops:
  8.0 2.4 %collective-permute-start = (bf16[4,768]{1,0:T(4,128)(2,1)S(1)}, bf16[4,768]{1,0:T(4,128)(2,1)S(1)}, u32[]{:S(2)}, u32[]{:S(2)}) collective-permute-start(bf16[4,768]{1,0:T(4,128)(2,1)S(1)} %get-tuple-element.16), channel_id=1, source_target_pairs={{0,1},{1,2},{2,3},{3,4},{4,5},{5,6},{6,7},{8,9},{9,10},{10,11},{11... | collective-permute-start | bytes 18440 | tf_op jit(solution)/shard_map/ppermute | solution.py:115
  10.4 1.3 collective-permute-start.1
  11.8 1.3 convert_reduce_fusion
  13.1 4.8 %fusion.32 = f32[1024,768]{1,0:T(8,128)} fusion(bf16[3,768,768]{2,1,0:T(8,128)(2,1)} %param.7, bf16[1,1024,768]{2,1,0:T(8,128)(2,1)} %param.6), kind=kOutput, calls=%fused_computation.38 | convolution fusion | flops 1207959552 | bytes 5898240 | tf_op jit(solution)/shard_map/dot_general | solution.py:140
  19.1 4.9 %fusion.19 = f32[1024,768]{1,0:T(8,128)} fusion(bf16[1024,768]{1,0:T(8,128)(2,1)} %bitcast.35, bf16[4,768]{1,0:T(4,128)(2,1)S(1)} %collective-permute-done, bf16[3,768,768]{2,1,0:T(8,128)(2,1)} %param.7), kind=kOutput, calls=%fused_computation.23 | convolution fusion | flops 1211105280 | bytes 5904384 | tf_op jit(solution)/shard_map/dot_general | solution.py:140
  24.0 8.9 %fusion.67 = (f32[768]{0:T(1024)S(1)}, f32[1024,768]{1,0:T(8,128)}) fusion(bf16[768,768]{1,0:T(8,128)(2,1)S(1)} %copy-done, f32[1024,768]{1,0:T(8,128)} %fusion.32, f32[1024,768]{1,0:T(8,128)} %fusion.19, bf16[4,768]{1,0:T(4,128)(2,1)S(1)} %collective-permute-done.1, bf16[1024,768]{1,0:T(8,128)(2,1)} %bitcast.36, f32[768]{0:T(1024)S(1)} %copy-done.5, ...), kind=kOutput, calls=%fused_computation.108 | convolution fusion | flops 2432433408 | bytes 13398016 | tf_op jit(solution)/shard_map/dot_general | solution.py:145
  33.6 17.7 %all-gather.1 = f32[8,1,896]{2,1,0:T(1,128)S(1)} all-gather(f32[1,1,896]{2,1,0:T(1,128)S(1)} %reshape.64), channel_id=2, replica_groups=mesh['view'=4,'tm'=8] {'tm'}, dimensions={0}, use_global_device_ids=true | all-gather | bytes 32256 | tf_op jit(solution)/shard_map/all_gather | solution.py:149
  55.7 2.4 %subtract_multiply_fusion = f32[1024,768]{1,0:T(8,128)S(1)} fusion(f32[1024,768]{1,0:T(8,128)} %get-tuple-element.22, f32[768]{0:T(1024)S(1)} %broadcast_divide_fusion.1, f32[1024]{0:T(1024)S(1)} %get-tuple-element.20), kind=kLoop, calls=%fused_computation.10 | loop fusion | flops 1572864 | bytes 6298624 | tf_op jit(solution)/shard_map/mul | solution.py:152
  58.2 1.7 convolution_dynamic-update-slice_fusion.8
  59.8 1.7 convolution_dynamic-update-slice_fusion.6
  61.6 2.0 fusion.39
  63.6 2.2 fusion.26
  65.7 2.6 %fusion.23 = f32[128,2688]{1,0:T(8,128)} fusion(f32[128,2688]{1,0:T(8,128)} %fusion.26, f32[1024,768]{1,0:T(8,128)S(1)} %subtract_multiply_fusion), kind=kOutput, calls=%fused_computation.32 | convolution fusion | flops 1006632960 | bytes 3473408 | tf_op jit(solution)/shard_map/dot_general | solution.py:21
  68.3 2.7 %convolution_dynamic-update-slice_fusion.1 = f32[128,2688]{1,0:T(8,128)} fusion(f32[128,2688]{1,0:T(8,128)} %fusion.23, f32[1024,768]{1,0:T(8,128)S(1)} %subtract_multiply_fusion), kind=kOutput, calls=%fused_computation.31 | convolution fusion | flops 1207959552 | bytes 4063232 | tf_op jit(solution)/shard_map/dot_general | solution.py:21
  74.7 57.9 %all-reduce.3.cloned.1.call-done = f32[128,2688]{1,0:T(8,128)} async-done(((f32[128,2688]{1,0:T(8,128)}), f32[128,2688]{1,0:T(8,128)}) %all-reduce.3.cloned.1.call-update) | async-done | bytes 1376272 | tf_op jit(solution)/shard_map/psum | solution.py:156
  132.5 2.6 %divide_add_fusion.gram_ref = f32[128,2688]{1,0:T(8,128)S(1)} fusion(f32[128,2688]{1,0:T(8,128)S(1)} %select_dynamic-update-slice_fusion, f32[128,2688]{1,0:T(8,128)} %all-reduce.3.cloned.1.call-done, f32[128,2688]{1,0:T(8,128)} %convolution_dynamic-update-slice_fusion, f32[]{:T(128)} %get-tuple-element.11), kind=kLoop, calls=%fused_computation.29 | loop fusion | flops 1032192 | bytes 5505028 | tf_op jit(solution)/shard_map/add | solution.py:166
  135.1 50.8 %shard_map.77 = f32[768,768]{1,0:T(8,128)S(1)} custom-call(f32[128,2688]{1,0:T(8,128)S(1)} %divide_add_fusion.gram_ref), custom_call_target="tpu_custom_call" | custom-call | tf_op jit(solution)/shard_map/pallas_call | solution.py:97
  186.0 8.1 %fusion.9 = f32[1024,768]{0,1:T(8,128)S(1)} fusion(f32[768,768]{1,0:T(8,128)S(1)} %shard_map.77, f32[1024,768]{1,0:T(8,128)S(1)} %copy-done.2, f32[768]{0:T(1024)S(1)} %broadcast_divide_fusion, f32[1024]{0:T(1024)S(1)} %get-tuple-element.20), kind=kOutput, calls=%fused_computation.11 | convolution fusion | flops 7249330176 | bytes 8657920 | tf_op jit(solution)/shard_map/dot_general | solution.py:21
  194.1 1.7 copy-done.1
  195.8 1.5 collective-permute-start.2
  197.4 16.3 %collective-permute-done.2 = bf16[512,768]{0,1:T(8,128)(2,1)S(1)} collective-permute-done((bf16[512,768]{0,1:T(8,128)(2,1)S(1)}, bf16[512,768]{0,1:T(8,128)(2,1)S(1)}, u32[]{:S(2)}, u32[]{:S(2)}) %collective-permute-start.2) | collective-permute-done | bytes 786464 | tf_op jit(solution)/shard_map/ppermute | solution.py:174
  213.7 1.7 multiply_reduce_fusion
  215.3 1.5 collective-permute-start.3
  216.8 3.5 %copy.15 = f32[1,1024,768]{2,1,0:T(8,128)} copy(f32[1,1024,768]{1,2,0:T(8,128)} %bitcast.29) | data formatting | bytes 6291456
  (46 shorter events, 10.8 us)
Async XLA Ops:
  7.2 16.8 %copy-start = (bf16[768,768]{1,0:T(8,128)(2,1)S(1)}, bf16[768,768]{1,0:T(8,128)(2,1)}, u32[]{:S(2)}) copy-start(bf16[768,768]{1,0:T(8,128)(2,1)} %param.9) | copy-start | bytes 3538948
  7.2 125.4 %all-reduce.3.cloned.1.call-start = ((), (), s32[]{:S(2)}) async-start(), calls=%async_computation | async-start | bytes 2752512 | tf_op jit(solution)/shard_map/psum | solution.py:156
  8.0 11.0 %collective-permute-start = (bf16[4,768]{1,0:T(4,128)(2,1)S(1)}, bf16[4,768]{1,0:T(4,128)(2,1)S(1)}, u32[]{:S(2)}, u32[]{:S(2)}) collective-permute-start(bf16[4,768]{1,0:T(4,128)(2,1)S(1)} %get-tuple-element.16), channel_id=1, source_target_pairs={{0,1},{1,2},{2,3},{3,4},{4,5},{5,6},{6,7},{8,9},{9,10},{10,11},{11... | collective-permute-start | bytes 18440 | tf_op jit(solution)/shard_map/ppermute | solution.py:115
  10.4 13.5 %collective-permute-start.1 = (bf16[4,768]{1,0:T(4,128)(2,1)S(1)}, bf16[4,768]{1,0:T(4,128)(2,1)S(1)}, u32[]{:S(2)}, u32[]{:S(2)}) collective-permute-start(bf16[4,768]{1,0:T(4,128)(2,1)S(1)} %get-tuple-element.15), channel_id=1, source_target_pairs={{1,0},{2,1},{3,2},{4,3},{5,4},{6,5},{7,6},{9,8},{10,9},{11,10},{12... | collective-permute-start | bytes 18440 | tf_op jit(solution)/shard_map/ppermute | solution.py:116
  13.1 5.3 %copy-start.3 = (s32[1024]{0:T(1024)S(1)}, s32[1024]{0:T(1024)}, u32[]{:S(2)}) copy-start(s32[1024]{0:T(1024)} %param.10) | copy-start | bytes 12292
  13.1 5.3 %copy-start.4 = (s32[1024]{0:T(1024)S(1)}, s32[1024]{0:T(1024)}, u32[]{:S(2)}) copy-start(s32[1024]{0:T(1024)} %param.11) | copy-start | bytes 12292
  19.1 4.9 %copy-start.5 = (f32[768]{0:T(1024)S(1)}, f32[768]{0:T(1024)}, u32[]{:S(2)}) copy-start(f32[768]{0:T(1024)} %param.8) | copy-start | bytes 9220
  135.1 50.8 %copy-start.2 = (f32[1024,768]{1,0:T(8,128)S(1)}, f32[1024,768]{1,0:T(8,128)}, u32[]{:S(2)}) copy-start(f32[1024,768]{1,0:T(8,128)} %get-tuple-element.22) | copy-start | bytes 9437188
  194.1 1.7 copy-start.1
  195.8 17.8 %collective-permute-start.2 = (bf16[512,768]{0,1:T(8,128)(2,1)S(1)}, bf16[512,768]{0,1:T(8,128)(2,1)S(1)}, u32[]{:S(2)}, u32[]{:S(2)}) collective-permute-start(bf16[512,768]{0,1:T(8,128)(2,1)S(1)} %dynamic-slice_convert_fusion), channel_id=1, source_target_pairs={{0,8},{8,0},{16,24},{24,16},{1,9},{9,1},{17,25},{25,17},{2,10},{10... | collective-permute-start | bytes 2359304 | tf_op jit(solution)/shard_map/ppermute | solution.py:174
  215.3 5.0 %collective-permute-start.3 = (f32[512]{0:T(512)S(1)}, f32[512]{0:T(512)S(1)}, u32[]{:S(2)}, u32[]{:S(2)}) collective-permute-start(f32[512]{0:T(512)S(1)} %broadcast_multiply_fusion), channel_id=1, source_target_pairs={{0,8},{8,0},{16,24},{24,16},{1,9},{9,1},{17,25},{25,17},{2,10},{10... | collective-permute-start | bytes 6152 | tf_op jit(solution)/shard_map/ppermute | solution.py:178
Sparse Core Ops, SparseCore 0:
  71.2 61.3 all-reduce.2

commit v2 on v1

--- a/solution.py
+++ b/solution.py
@@ -108,6 +108,120 @@
     )(packed)
 
 
+def reduce_kernel(n, chunks, x_ref, stats_ref, out_ref, all_ref, half_in, half, quarter_in, quarter,
+                  far_in, send_sem, recv_sem, stat_send, stat_recv):
+    me = lax.axis_index("tm")
+    levels = n.bit_length() - 1
+    rows = x_ref.shape[0] // chunks
+    h, q = rows // 2, rows // 4
+    bit0, bit1 = lax.rem(me, 2), lax.rem(me // 2, 2)
+
+    def across(level):
+        size = 2**level
+        return me + size * (1 - 2 * lax.rem(me // size, 2))
+
+    barrier = pltpu.get_barrier_semaphore()
+    for d in range(1, n):
+        pl.semaphore_signal(
+            barrier, inc=1, device_id={"tm": lax.rem(me + d, n)}, device_id_type=pl.DeviceIdType.MESH
+        )
+    pl.semaphore_wait(barrier, n - 1)
+
+    def copy(src, dst, peer, ssem, rsem):
+        c = pltpu.make_async_remote_copy(
+            src_ref=src,
+            dst_ref=dst,
+            send_sem=ssem,
+            recv_sem=rsem,
+            device_id={"tm": peer},
+            device_id_type=pl.DeviceIdType.MESH,
+        )
+        c.start()
+        return c
+
+    def part(start, size):
+        return pl.ds(pl.multiple_of(start, q), size)
+
+    flight = {}
+    stages = levels + 2
+
+    def step(c, stage):
+        if stage:
+            flight[c].wait()
+        s0 = c * rows + bit0 * h
+        s1 = s0 + bit1 * q
+        mine = part(s1, q)
+        if stage == 1:
+            half[c] = x_ref[part(s0, h), :] + half_in[c]
+        elif stage == 2:
+            quarter[0, c] = half[c, part(bit1 * q, q), :] + quarter_in[c]
+        elif 2 < stage < levels:
+            quarter[stage - 2, c] = quarter[stage - 3, c] + far_in[stage - 3, c]
+        elif stage == levels:
+            out_ref[mine, :] = quarter[levels - 3, c] + far_in[levels - 3, c]
+        if stage == stages:
+            return
+        if stage == 0:
+            src, dst, peer = x_ref.at[part(c * rows + (1 - bit0) * h, h)], half_in.at[c], across(0)
+        elif stage == 1:
+            src, dst, peer = half.at[c, part((1 - bit1) * q, q)], quarter_in.at[c], across(1)
+        elif stage < levels:
+            src, dst, peer = quarter.at[stage - 2, c], far_in.at[stage - 2, c], across(stage)
+        elif stage == levels:
+            src, dst, peer = out_ref.at[mine], out_ref.at[mine], across(1)
+        else:
+            own = part(s0, h)
+            src, dst, peer = out_ref.at[own], out_ref.at[own], across(0)
+        flight[c] = copy(src, dst, peer, send_sem.at[stage, c], recv_sem.at[stage, c])
+
+    for c in range(chunks):
+        step(c, 0)
+    all_ref[me] = stats_ref[...]
+    gathers = [
+        copy(stats_ref, all_ref.at[me], lax.rem(me + d, n), stat_send.at[d], stat_recv.at[d])
+        for d in range(1, n)
+    ]
+    for t in range(1, chunks + stages):
+        for c in range(chunks):
+            if 1 <= t - c <= stages:
+                step(c, t - c)
+    for g in gathers:
+        g.wait()
+
+
+def reduce_and_gather(packed, stats, n):
+    assert n >= 8 and n & (n - 1) == 0
+    chunks = 4
+    levels = n.bit_length() - 1
+    height, width = packed.shape
+    h, q = height // chunks // 2, height // chunks // 4
+    f32 = jnp.float32
+    vmem = pl.BlockSpec(memory_space=pltpu.VMEM)
+    return pl.pallas_call(
+        functools.partial(reduce_kernel, n, chunks),
+        out_shape=(
+            jax.ShapeDtypeStruct((height, width), f32),
+            jax.ShapeDtypeStruct((n,) + stats.shape, f32),
+        ),
+        in_specs=[vmem] * 2,
+        out_specs=(vmem, vmem),
+        scratch_shapes=[
+            pltpu.VMEM((chunks, h, width), f32),
+            pltpu.VMEM((chunks, h, width), f32),
+            pltpu.VMEM((chunks, q, width), f32),
+            pltpu.VMEM((levels - 2, chunks, q, width), f32),
+            pltpu.VMEM((levels - 2, chunks, q, width), f32),
+            pltpu.SemaphoreType.DMA((levels + 2, chunks)),
+            pltpu.SemaphoreType.DMA((levels + 2, chunks)),
+            pltpu.SemaphoreType.DMA((n,)),
+            pltpu.SemaphoreType.DMA((n,)),
+        ],
+        compiler_params=pltpu.CompilerParams(
+            collective_id=0, has_side_effects=True, vmem_limit_bytes=32 * 1024 * 1024
+        ),
+    )(packed, stats)
+
+
 def padded(shard, axis, width):
     count, length = (lax.axis_size(axis), shard.shape[0])
     up = [(i, (i + 1) % count) for i in range(count - 1)]
@@ -146,14 +260,17 @@
 
     local_count = jnp.sum(live)
     local_mean = jnp.sum(embed, axis=0) / jnp.maximum(local_count, 1.0)
-    stats = lax.all_gather(
-        jnp.concatenate([local_mean, jnp.broadcast_to(local_count, (B,))]), "tm"
+    stats = jnp.concatenate([local_mean, jnp.broadcast_to(local_count, (B,))])[None]
+    about = live[:, None] * (embed - local_mean[None, :])
+    pair = 2 * B
+    bands = [
+        dot(about[:, i * pair : (i + 1) * pair], about[:, : (i + 1) * pair], TN) for i in range(n // 2)
+    ]
+    gram = lower_blocks(
+        lambda i: bands[i // 2][(i % 2) * B : (i % 2 + 1) * B, : (i + 1) * B], n
     )
-    about = live[:, None] * (embed - local_mean[None, :])
-    gram = lower_blocks(
-        lambda i: dot(about[:, i * B : (i + 1) * B], about[:, : (i + 1) * B], TN), n
-    )
-    gram = lax.psum(gram, "tm")
+    gram, stats = reduce_and_gather(gram, stats, lax.axis_size("tm"))
+    stats = stats[:, 0]
     counts = stats[:, width]
     means = stats[:, :width]
     count = jnp.sum(counts)

time: 228 us -> 170 us (0.75)
  waiting for transfers between devices: 74.2 us -> 18.3 us
  Pallas kernels: 50.8 us -> 91.3 us
  blocking collectives: 17.7 us -> 0 us
  between operations: 14.9 us -> 1.66 us
  matrix products: 46.2 us -> 36.4 us
    psum x1 -> x0, waiting for transfers between devices: 57.9 us -> none  [per_device(): gram = lax.psum(gram, 'tm')]
    pallas_call x0 -> x1, Pallas kernels: none -> 40.7 us  [reduce_and_gather(): pl.pallas_call(functools.partial(reduce_kernel, n, chunks), out_shape=(ja...]
    all_gather x1 -> x0, blocking collectives: 17.7 us -> none  [per_device(): lax.all_gather(jnp.concatenate([local_mean, jnp.broadcast_to(local_count,...]
    dot_general x13 -> x10, matrix products: 27.6 us -> 17.8 us  [dot(): lax.dot_general(a, b, dims, precision=precision, preferred_element_type=j...]
    unnamed x15 -> x19, local copies, waits for them, and re-layouts: 5.23 us -> 5.31 us
  transfers between devices with their start and end apart: 5 -> 4, of which waited for: 2 -> 1; matrix products, arithmetic and copies ran while one was open for 8% -> 9% of each run, Pallas kernels for 0% -> 0%
where the time goes in v2:
time: 170 us
  Pallas kernels  91.3 us (54%)
  matrix products  36.4 us (21%)
  waiting for transfers between devices  18.3 us (11%)
  other arithmetic  8.79 us (5%)
  local copies, waits for them, and re-layouts  6.94 us (4%)
  starting transfers between devices  6.76 us (4%)
    pallas_call x1, Pallas kernels, inverse_factor(): pl.pallas_call(functools.partial(factor_kernel, n), out_shape=jax.ShapeDt...  50.6 us
    pallas_call x1, Pallas kernels, reduce_and_gather(): pl.pallas_call(functools.partial(reduce_kernel, n, chunks), out_shape=(ja...  40.7 us
    ppermute x1, waiting for transfers between devices, per_device(): partner = lax.ppermute(sent, 'view', pairs).astype(jnp.float32)  18.3 us
    dot_general x10, matrix products, dot(): lax.dot_general(a, b, dims, precision=precision, preferred_element_type=j...  17.8 us
    dot_general x2, matrix products, per_device(): jnp.dot(shifted_input, conv_weight[frame_index], preferred_element_type=j...  9.65 us
    dot_general x1, matrix products, per_device(): embed = jnp.dot(hidden, proj_weight, preferred_element_type=jnp.float32)  8.96 us
    unnamed x19, local copies, waits for them, and re-layouts  5.31 us
  transfers between devices with their start and end apart: 4, of which 1 were waited for; matrix products, arithmetic and copies ran while one was open for 9% of the time, Pallas kernels for 0%

profile of v2, /device:TPU:0, one launch (start us, length us, event | category | flops | bytes accessed | tf_op | source)
XLA Modules:
  0.0 170.1 jit_solution(8342198652847916309)
XLA Ops:
  0.6 0.8 slice_bitcast_fusion
  1.5 2.4 %collective-permute-start = (bf16[4,768]{1,0:T(4,128)(2,1)S(1)}, bf16[4,768]{1,0:T(4,128)(2,1)S(1)}, u32[]{:S(2)}, u32[]{:S(2)}) collective-permute-start(bf16[4,768]{1,0:T(4,128)(2,1)S(1)} %get-tuple-element.16), channel_id=1, source_target_pairs={{0,1},{1,2},{2,3},{3,4},{4,5},{5,6},{6,7},{8,9},{9,10},{10,11},{11... | collective-permute-start | bytes 18440 | tf_op jit(solution)/shard_map/ppermute | solution.py:229
  3.8 1.3 collective-permute-start.1
  5.2 1.3 convert_reduce_fusion
  6.5 4.8 %fusion.22 = f32[1024,768]{1,0:T(8,128)} fusion(bf16[3,768,768]{2,1,0:T(8,128)(2,1)} %param.7, bf16[1,1024,768]{2,1,0:T(8,128)(2,1)} %param.6), kind=kOutput, calls=%fused_computation.31 | convolution fusion | flops 1207959552 | bytes 5898240 | tf_op jit(solution)/shard_map/dot_general | solution.py:254
  12.5 4.8 %fusion.15 = f32[1024,768]{1,0:T(8,128)} fusion(bf16[1024,768]{1,0:T(8,128)(2,1)} %bitcast.35, bf16[4,768]{1,0:T(4,128)(2,1)S(1)} %collective-permute-done, bf16[3,768,768]{2,1,0:T(8,128)(2,1)} %param.7), kind=kOutput, calls=%fused_computation.19 | convolution fusion | flops 1211105280 | bytes 5904384 | tf_op jit(solution)/shard_map/dot_general | solution.py:254
  17.4 9.0 %fusion.52 = (f32[768]{0:T(1024)S(1)}, f32[1024,768]{1,0:T(8,128)}) fusion(bf16[768,768]{1,0:T(8,128)(2,1)S(1)} %copy-done, f32[1024,768]{1,0:T(8,128)} %fusion.22, f32[1024,768]{1,0:T(8,128)} %fusion.15, bf16[4,768]{1,0:T(4,128)(2,1)S(1)} %collective-permute-done.1, bf16[1024,768]{1,0:T(8,128)(2,1)} %bitcast.36, f32[768]{0:T(1024)S(1)} %copy-done.5, ...), kind=kOutput, calls=%fused_computation.102 | convolution fusion | flops 2432433408 | bytes 13398016 | tf_op jit(solution)/shard_map/dot_general | solution.py:259
  26.3 2.4 %subtract_multiply_fusion = f32[1024,768]{1,0:T(8,128)S(1)} fusion(f32[1024,768]{1,0:T(8,128)} %get-tuple-element.22, f32[768]{0:T(1024)S(1)} %broadcast_divide_fusion.1, f32[1024]{0:T(1024)S(1)} %get-tuple-element.20), kind=kLoop, calls=%fused_computation.13 | loop fusion | flops 1572864 | bytes 6298624 | tf_op jit(solution)/shard_map/mul | solution.py:264
  28.7 1.9 %fusion.32 = f32[256,256]{1,0:T(8,128)S(1)} fusion(f32[1024,768]{1,0:T(8,128)S(1)} %subtract_multiply_fusion), kind=kOutput, calls=%fused_computation.43 | convolution fusion | flops 805306368 | bytes 1310720 | tf_op jit(solution)/shard_map/dot_general | solution.py:21
  30.7 2.1 %fusion.12 = f32[256,512]{1,0:T(8,128)S(1)} fusion(f32[1024,768]{1,0:T(8,128)S(1)} %subtract_multiply_fusion), kind=kOutput, calls=%fused_computation.14 | convolution fusion | flops 1610612736 | bytes 3670016 | tf_op jit(solution)/shard_map/dot_general | solution.py:21
  32.7 3.2 %fusion.29 = f32[256,768]{1,0:T(8,128)S(1)} fusion(f32[1024,768]{1,0:T(8,128)S(1)} %subtract_multiply_fusion), kind=kOutput, calls=%fused_computation.40 | convolution fusion | flops 2415919104 | bytes 4980736 | tf_op jit(solution)/shard_map/dot_general | solution.py:21
  36.0 0.7 concatenate.46
  36.8 40.7 %shard_map.77 = (f32[128,2688]{1,0:T(8,128)S(1)}, f32[8,1,896]{2,1,0:T(1,128)S(1)}) custom-call(f32[128,2688]{1,0:T(8,128)S(1)} %slice_dynamic-update-slice_fusion.x_ref, f32[1,896]{1,0:T(1,128)S(1)} %broadcast_in_dim.4.stats_ref), custom_call_target="tpu_custom_call" | custom-call | tf_op jit(solution)/shard_map/pallas_call | solution.py:200
  77.5 0.6 sqrt_reduce_fusion
  78.2 0.7 broadcast_divide_fusion
  81.4 0.9 divide_add_fusion.gram_ref
  82.3 50.6 %shard_map.78 = f32[768,768]{1,0:T(8,128)S(1)} custom-call(f32[128,2688]{1,0:T(8,128)S(1)} %divide_add_fusion.gram_ref), custom_call_target="tpu_custom_call" | custom-call | tf_op jit(solution)/shard_map/pallas_call | solution.py:97
  132.9 8.2 %fusion.9 = f32[1024,768]{0,1:T(8,128)S(1)} fusion(f32[768,768]{1,0:T(8,128)S(1)} %shard_map.78, f32[1024,768]{1,0:T(8,128)S(1)} %copy-done.2, f32[768]{0:T(1024)S(1)} %broadcast_divide_fusion, f32[1024]{0:T(1024)S(1)} %get-tuple-element.20), kind=kOutput, calls=%fused_computation.10 | convolution fusion | flops 7249330176 | bytes 8657920 | tf_op jit(solution)/shard_map/dot_general | solution.py:21
  141.1 1.7 copy-done.1
  142.9 1.6 collective-permute-start.2
  144.4 18.3 %collective-permute-done.2 = bf16[512,768]{0,1:T(8,128)(2,1)S(1)} collective-permute-done((bf16[512,768]{0,1:T(8,128)(2,1)S(1)}, bf16[512,768]{0,1:T(8,128)(2,1)S(1)}, u32[]{:S(2)}, u32[]{:S(2)}) %collective-permute-start.2) | collective-permute-done | bytes 786464 | tf_op jit(solution)/shard_map/ppermute | solution.py:291
  162.7 1.7 multiply_reduce_fusion
  164.4 1.6 collective-permute-start.3
  166.0 3.5 %copy.13 = f32[1,1024,768]{2,1,0:T(8,128)} copy(f32[1,1024,768]{1,2,0:T(8,128)} %bitcast.29) | data formatting | bytes 6291456
  (46 shorter events, 3.9 us)
Async XLA Ops:
  0.6 16.7 %copy-start = (bf16[768,768]{1,0:T(8,128)(2,1)S(1)}, bf16[768,768]{1,0:T(8,128)(2,1)}, u32[]{:S(2)}) copy-start(bf16[768,768]{1,0:T(8,128)(2,1)} %param.9) | copy-start | bytes 3538948
  1.5 11.0 %collective-permute-start = (bf16[4,768]{1,0:T(4,128)(2,1)S(1)}, bf16[4,768]{1,0:T(4,128)(2,1)S(1)}, u32[]{:S(2)}, u32[]{:S(2)}) collective-permute-start(bf16[4,768]{1,0:T(4,128)(2,1)S(1)} %get-tuple-element.16), channel_id=1, source_target_pairs={{0,1},{1,2},{2,3},{3,4},{4,5},{5,6},{6,7},{8,9},{9,10},{10,11},{11... | collective-permute-start | bytes 18440 | tf_op jit(solution)/shard_map/ppermute | solution.py:229
  3.8 13.5 %collective-permute-start.1 = (bf16[4,768]{1,0:T(4,128)(2,1)S(1)}, bf16[4,768]{1,0:T(4,128)(2,1)S(1)}, u32[]{:S(2)}, u32[]{:S(2)}) collective-permute-start(bf16[4,768]{1,0:T(4,128)(2,1)S(1)} %get-tuple-element.15), channel_id=1, source_target_pairs={{1,0},{2,1},{3,2},{4,3},{5,4},{6,5},{7,6},{9,8},{10,9},{11,10},{12... | collective-permute-start | bytes 18440 | tf_op jit(solution)/shard_map/ppermute | solution.py:230
  6.5 5.3 %copy-start.3 = (s32[1024]{0:T(1024)S(1)}, s32[1024]{0:T(1024)}, u32[]{:S(2)}) copy-start(s32[1024]{0:T(1024)} %param.10) | copy-start | bytes 12292
  6.5 5.3 %copy-start.4 = (s32[1024]{0:T(1024)S(1)}, s32[1024]{0:T(1024)}, u32[]{:S(2)}) copy-start(s32[1024]{0:T(1024)} %param.11) | copy-start | bytes 12292
  12.5 4.8 %copy-start.5 = (f32[768]{0:T(1024)S(1)}, f32[768]{0:T(1024)}, u32[]{:S(2)}) copy-start(f32[768]{0:T(1024)} %param.8) | copy-start | bytes 9220
  82.3 50.6 %copy-start.2 = (f32[1024,768]{1,0:T(8,128)S(1)}, f32[1024,768]{1,0:T(8,128)}, u32[]{:S(2)}) copy-start(f32[1024,768]{1,0:T(8,128)} %get-tuple-element.22) | copy-start | bytes 9437188
  141.1 1.7 copy-start.1
  142.9 19.9 %collective-permute-start.2 = (bf16[512,768]{0,1:T(8,128)(2,1)S(1)}, bf16[512,768]{0,1:T(8,128)(2,1)S(1)}, u32[]{:S(2)}, u32[]{:S(2)}) collective-permute-start(bf16[512,768]{0,1:T(8,128)(2,1)S(1)} %dynamic-slice_convert_fusion), channel_id=1, source_target_pairs={{0,8},{8,0},{16,24},{24,16},{1,9},{9,1},{17,25},{25,17},{2,10},{10... | collective-permute-start | bytes 2359304 | tf_op jit(solution)/shard_map/ppermute | solution.py:291
  164.4 5.1 %collective-permute-start.3 = (f32[512]{0:T(512)S(1)}, f32[512]{0:T(512)S(1)}, u32[]{:S(2)}, u32[]{:S(2)}) collective-permute-start(f32[512]{0:T(512)S(1)} %broadcast_multiply_fusion), channel_id=1, source_target_pairs={{0,8},{8,0},{16,24},{24,16},{1,9},{9,1},{17,25},{25,17},{2,10},{10... | collective-permute-start | bytes 6152 | tf_op jit(solution)/shard_map/ppermute | solution.py:295

commit v3 on v2

--- a/solution.py
+++ b/solution.py
@@ -281,17 +281,30 @@
     )
     ridge = lower_blocks(lambda i: eps_shrink * jnp.eye(B, (i + 1) * B, i * B, dtype=jnp.float32), n)
     inverse = inverse_factor((gram + between) / count + ridge, width)
-    centered = live[:, None] * (embed - mean[None, :])
-    whitened = dot(centered, inverse, NT)
+
+    def whiten(start, size):
+        rows = lax.dynamic_slice_in_dim(embed, start, size)
+        here = lax.dynamic_slice_in_dim(live, start, size)
+        return dot(here[:, None] * (rows - mean[None, :]), inverse, NT)
 
     half = frame_rows // 2
+    piece = half // 2
     bit = lax.axis_index("view") % 2
     pairs = [(i, i ^ 1) for i in range(lax.axis_size("view"))]
-    sent = lax.dynamic_slice_in_dim(whitened, (1 - bit) * half, half).astype(jnp.bfloat16)
-    partner = lax.ppermute(sent, "view", pairs).astype(jnp.float32)
-    own = lax.dynamic_slice_in_dim(whitened, bit * half, half)
-    diff = own - partner
-    mine = jnp.sum(diff * diff, axis=1) / width
+    whitened = jnp.zeros((frame_rows, width), jnp.float32)
+    arrived = []
+    for k in range(2):
+        start = (1 - bit) * half + k * piece
+        first = whiten(start, piece)
+        arrived.append(lax.ppermute(first.astype(jnp.bfloat16), "view", pairs))
+        whitened = lax.dynamic_update_slice_in_dim(whitened, first, start, 0)
+    own = whiten(bit * half, half)
+    whitened = lax.dynamic_update_slice_in_dim(whitened, own, bit * half, 0)
+    losses = []
+    for k in range(2):
+        diff = own[k * piece : (k + 1) * piece] - arrived[k].astype(jnp.float32)
+        losses.append(jnp.sum(diff * diff, axis=1) / width)
+    mine = jnp.concatenate(losses)
     theirs = lax.ppermute(mine, "view", pairs)
     pair_loss = jnp.where(bit == 0, jnp.concatenate([mine, theirs]), jnp.concatenate([theirs, mine]))
     return (whitened[None], pair_loss[None])

time: 170 us -> 169 us (level)
  waiting for transfers between devices: 18.3 us -> 13.5 us
  matrix products: 36.4 us -> 40.7 us
    ppermute x1 -> x2, waiting for transfers between devices: 18.3 us -> 11.4 us  [per_device(): arrived.append(lax.ppermute(first.astype(jnp.bfloat16), 'view', pairs))]
    dot_general x10 -> x12, matrix products: 17.8 us -> 22.1 us  [dot(): lax.dot_general(a, b, dims, precision=precision, preferred_element_type=j...]
    ppermute x1, waiting for transfers between devices: 0.01 us -> 2.1 us  [per_device(): theirs = lax.ppermute(mine, 'view', pairs)]
    unnamed x19 -> x18, local copies, waits for them, and re-layouts: 5.31 us -> 3.44 us
  transfers between devices with their start and end apart: 4 -> 5, of which waited for: 1 -> 3; matrix products, arithmetic and copies ran while one was open for 9% -> 11% of each run, Pallas kernels for 0% -> 0%
where the time goes in v3:
time: 169 us; the launch traced here: 168 us
  Pallas kernels  90.5 us (54%)
  matrix products  40.7 us (24%)
  waiting for transfers between devices  13.5 us (8%)
  other arithmetic  8.54 us (5%)
  starting transfers between devices  7.91 us (5%)
  local copies, waits for them, and re-layouts  5.32 us (3%)
    pallas_call x1, Pallas kernels, inverse_factor(): pl.pallas_call(functools.partial(factor_kernel, n), out_shape=jax.ShapeDt...  50.6 us
    pallas_call x1, Pallas kernels, reduce_and_gather(): pl.pallas_call(functools.partial(reduce_kernel, n, chunks), out_shape=(ja...  40 us
    dot_general x12, matrix products, dot(): lax.dot_general(a, b, dims, precision=precision, preferred_element_type=j...  22.1 us
    ppermute x2, waiting for transfers between devices, per_device(): arrived.append(lax.ppermute(first.astype(jnp.bfloat16), 'view', pairs))  11.4 us
    dot_general x2, matrix products, per_device(): jnp.dot(shifted_input, conv_weight[frame_index], preferred_element_type=j...  9.69 us
    dot_general x1, matrix products, per_device(): embed = jnp.dot(hidden, proj_weight, preferred_element_type=jnp.float32)  8.92 us
    unnamed x18, local copies, waits for them, and re-layouts  3.44 us
  transfers between devices with their start and end apart: 5, of which 3 were waited for; matrix products, arithmetic and copies ran while one was open for 11% of the time, Pallas kernels for 0%

profile of v3, /device:TPU:0, one launch (start us, length us, event | category | flops | bytes accessed | tf_op | source)
XLA Modules:
  0.0 168.1 jit_solution(2740693298864237336)
XLA Ops:
  1.5 1.3 collective-permute-start.1
  2.8 3.0 %collective-permute-start = (bf16[4,768]{1,0:T(4,128)(2,1)S(1)}, bf16[4,768]{1,0:T(4,128)(2,1)S(1)}, u32[]{:S(2)}, u32[]{:S(2)}) collective-permute-start(bf16[4,768]{1,0:T(4,128)(2,1)S(1)} %get-tuple-element.14), channel_id=1, source_target_pairs={{0,1},{1,2},{2,3},{3,4},{4,5},{5,6},{6,7},{8,9},{9,10},{10,11},{11... | collective-permute-start | bytes 18440 | tf_op jit(solution)/shard_map/ppermute | solution.py:229
  5.9 1.3 convert_reduce_fusion
  7.2 4.8 %fusion.21 = f32[1024,768]{1,0:T(8,128)} fusion(bf16[3,768,768]{2,1,0:T(8,128)(2,1)} %param.7, bf16[1,1024,768]{2,1,0:T(8,128)(2,1)} %param.6), kind=kOutput, calls=%fused_computation.29 | convolution fusion | flops 1207959552 | bytes 5898240 | tf_op jit(solution)/shard_map/dot_general | solution.py:254
  13.3 4.9 %fusion.12 = f32[1024,768]{1,0:T(8,128)} fusion(bf16[1024,768]{1,0:T(8,128)(2,1)} %bitcast.43, bf16[4,768]{1,0:T(4,128)(2,1)S(1)} %collective-permute-done, bf16[3,768,768]{2,1,0:T(8,128)(2,1)} %param.7), kind=kOutput, calls=%fused_computation.16 | convolution fusion | flops 1211105280 | bytes 5904384 | tf_op jit(solution)/shard_map/dot_general | solution.py:254
  18.1 8.9 %fusion.73 = (f32[768]{0:T(1024)S(1)}, f32[1024,768]{1,0:T(8,128)}) fusion(bf16[768,768]{1,0:T(8,128)(2,1)S(1)} %copy-done, f32[1024,768]{1,0:T(8,128)} %fusion.21, f32[1024,768]{1,0:T(8,128)} %fusion.12, bf16[4,768]{1,0:T(4,128)(2,1)S(1)} %collective-permute-done.1, bf16[1024,768]{1,0:T(8,128)(2,1)} %bitcast.44, f32[768]{0:T(1024)S(1)} %copy-done.5, ...), kind=kOutput, calls=%fused_computation.128 | convolution fusion | flops 2432433408 | bytes 13398016 | tf_op jit(solution)/shard_map/dot_general | solution.py:259
  27.7 2.4 %subtract_multiply_fusion = f32[1024,768]{1,0:T(8,128)S(1)} fusion(f32[1024,768]{1,0:T(8,128)} %get-tuple-element.22, f32[768]{0:T(1024)S(1)} %broadcast_divide_fusion.1, f32[1024]{0:T(1024)S(1)} %get-tuple-element.20), kind=kLoop, calls=%fused_computation.10 | loop fusion | flops 1572864 | bytes 6298624 | tf_op jit(solution)/shard_map/mul | solution.py:264
  30.1 1.9 %fusion.31 = f32[256,256]{1,0:T(8,128)S(1)} fusion(f32[1024,768]{1,0:T(8,128)S(1)} %subtract_multiply_fusion), kind=kOutput, calls=%fused_computation.41 | convolution fusion | flops 805306368 | bytes 1310720 | tf_op jit(solution)/shard_map/dot_general | solution.py:21
  32.0 2.1 %fusion.9 = f32[256,512]{1,0:T(8,128)S(1)} fusion(f32[1024,768]{1,0:T(8,128)S(1)} %subtract_multiply_fusion), kind=kOutput, calls=%fused_computation.11 | convolution fusion | flops 1610612736 | bytes 3670016 | tf_op jit(solution)/shard_map/dot_general | solution.py:21
  34.1 3.2 %fusion.28 = f32[256,768]{1,0:T(8,128)S(1)} fusion(f32[1024,768]{1,0:T(8,128)S(1)} %subtract_multiply_fusion), kind=kOutput, calls=%fused_computation.38 | convolution fusion | flops 2415919104 | bytes 4980736 | tf_op jit(solution)/shard_map/dot_general | solution.py:21
  37.5 40.0 %shard_map.77 = (f32[128,2688]{1,0:T(8,128)S(1)}, f32[8,1,896]{2,1,0:T(1,128)S(1)}) custom-call(f32[128,2688]{1,0:T(8,128)S(1)} %slice_dynamic-update-slice_fusion.x_ref, f32[1,896]{1,0:T(1,128)S(1)} %broadcast_in_dim.11.stats_ref), custom_call_target="tpu_custom_call" | custom-call | tf_op jit(solution)/shard_map/pallas_call | solution.py:200
  81.4 0.9 divide_add_fusion.gram_ref
  82.3 50.6 %shard_map.78 = f32[768,768]{1,0:T(8,128)S(1)} custom-call(f32[128,2688]{1,0:T(8,128)S(1)} %divide_add_fusion.gram_ref), custom_call_target="tpu_custom_call" | custom-call | tf_op jit(solution)/shard_map/pallas_call | solution.py:97
  133.1 1.7 copy-done.1
  134.7 3.0 %bitcast_dynamic-update-slice_fusion.2 = (f32[1,1024,768]{2,1,0:T(8,128)S(1)}, bf16[256,768]{1,0:T(8,128)(2,1)}) fusion(f32[1,1024,768]{2,1,0:T(8,128)S(1)} %broadcast_in_dim.10, s32[]{:T(128)S(6)} %select_n.38, f32[768,768]{1,0:T(8,128)S(1)} %shard_map.78, f32[1024,768]{1,0:T(8,128)S(1)} %copy-done.1, f32[768]{0:T(1024)S(1)} %broadcast_divide_fusion, ...), kind=kOutput, calls=%fused_computation.50 | convolution fusion | flops 1812529152 | bytes 4331520 | tf_op jit(solution)/shard_map/dot_general | solution.py:21
  137.7 3.0 %bitcast_dynamic-update-slice_fusion.1 = (f32[1,1024,768]{2,1,0:T(8,128)S(1)}, bf16[256,768]{1,0:T(8,128)(2,1)}) fusion(f32[1,1024,768]{2,1,0:T(8,128)S(1)} %get-tuple-element.23, s32[]{:T(128)S(6)} %select_n.39, f32[768,768]{1,0:T(8,128)S(1)} %shard_map.78, f32[1024,768]{1,0:T(8,128)S(1)} %copy-done.1, f32[256]{0:T(256)S(1)} %get-tuple-element.17, ...), kind=kOutput, calls=%fused_computation.49 | convolution fusion | flops 1812529152 | bytes 4331520 | tf_op jit(solution)/shard_map/dot_general | solution.py:21
  140.6 1.7 copy-done.2
  142.3 1.5 collective-permute-start.3
  144.4 6.6 %bitcast_dynamic-update-slice_fusion = (f32[1,1024,768]{2,1,0:T(8,128)}, f32[512,768]{1,0:T(8,128)S(1)}) fusion(f32[1,1024,768]{2,1,0:T(8,128)} %copy-done.2, s32[]{:T(128)S(6)} %select_n.40, f32[768,768]{1,0:T(8,128)S(1)} %shard_map.78, f32[1024,768]{1,0:T(8,128)} %get-tuple-element.22, f32[768]{0:T(1024)S(1)} %broadcast_divide_fusion, ...), kind=kOutput, calls=%fused_computation.18 | convolution fusion | flops 3624665088 | bytes 7084032 | tf_op jit(solution)/shard_map/dot_general | solution.py:21
  151.0 3.5 %collective-permute-done.3 = bf16[256,768]{1,0:T(8,128)(2,1)} collective-permute-done((bf16[256,768]{1,0:T(8,128)(2,1)}, bf16[256,768]{1,0:T(8,128)(2,1)}, u32[]{:S(2)}, u32[]{:S(2)}) %collective-permute-start.3) | collective-permute-done | bytes 393248 | tf_op jit(solution)/shard_map/ppermute | solution.py:299
  154.6 7.9 %collective-permute-done.2 = bf16[256,768]{1,0:T(8,128)(2,1)} collective-permute-done((bf16[256,768]{1,0:T(8,128)(2,1)}, bf16[256,768]{1,0:T(8,128)(2,1)}, u32[]{:S(2)}, u32[]{:S(2)}) %collective-permute-start.2) | collective-permute-done | bytes 393248 | tf_op jit(solution)/shard_map/ppermute | solution.py:299
  162.4 1.4 fusion.36
  163.9 1.6 collective-permute-start.4
  165.4 2.1 %collective-permute-done.4 = f32[512]{0:T(512)S(1)} collective-permute-done((f32[512]{0:T(512)S(1)}, f32[512]{0:T(512)S(1)}, u32[]{:S(2)}, u32[]{:S(2)}) %collective-permute-start.4) | collective-permute-done | bytes 2080 | tf_op jit(solution)/shard_map/ppermute | solution.py:308
  (52 shorter events, 7.4 us)
Async XLA Ops:
  0.6 17.5 %copy-start = (bf16[768,768]{1,0:T(8,128)(2,1)S(1)}, bf16[768,768]{1,0:T(8,128)(2,1)}, u32[]{:S(2)}) copy-start(bf16[768,768]{1,0:T(8,128)(2,1)} %param.9) | copy-start | bytes 3538948
  1.5 16.7 %collective-permute-start.1 = (bf16[4,768]{1,0:T(4,128)(2,1)S(1)}, bf16[4,768]{1,0:T(4,128)(2,1)S(1)}, u32[]{:S(2)}, u32[]{:S(2)}) collective-permute-start(bf16[4,768]{1,0:T(4,128)(2,1)S(1)} %get-tuple-element.13), channel_id=1, source_target_pairs={{1,0},{2,1},{3,2},{4,3},{5,4},{6,5},{7,6},{9,8},{10,9},{11,10},{12... | collective-permute-start | bytes 18440 | tf_op jit(solution)/shard_map/ppermute | solution.py:230
  2.8 10.5 %collective-permute-start = (bf16[4,768]{1,0:T(4,128)(2,1)S(1)}, bf16[4,768]{1,0:T(4,128)(2,1)S(1)}, u32[]{:S(2)}, u32[]{:S(2)}) collective-permute-start(bf16[4,768]{1,0:T(4,128)(2,1)S(1)} %get-tuple-element.14), channel_id=1, source_target_pairs={{0,1},{1,2},{2,3},{3,4},{4,5},{5,6},{6,7},{8,9},{9,10},{10,11},{11... | collective-permute-start | bytes 18440 | tf_op jit(solution)/shard_map/ppermute | solution.py:229
  7.2 4.8 %copy-start.3 = (s32[1024]{0:T(1024)S(1)}, s32[1024]{0:T(1024)}, u32[]{:S(2)}) copy-start(s32[1024]{0:T(1024)} %param.10) | copy-start | bytes 12292
  7.2 4.8 %copy-start.4 = (s32[1024]{0:T(1024)S(1)}, s32[1024]{0:T(1024)}, u32[]{:S(2)}) copy-start(s32[1024]{0:T(1024)} %param.11) | copy-start | bytes 12292
  13.3 4.9 %copy-start.5 = (f32[768]{0:T(1024)S(1)}, f32[768]{0:T(1024)}, u32[]{:S(2)}) copy-start(f32[768]{0:T(1024)} %param.8) | copy-start | bytes 9220
  132.9 1.9 %copy-start.1 = (f32[1024,768]{1,0:T(8,128)S(1)}, f32[1024,768]{1,0:T(8,128)}, u32[]{:S(2)}) copy-start(f32[1024,768]{1,0:T(8,128)} %get-tuple-element.22) | copy-start | bytes 9437188
  140.6 1.7 copy-start.2
  142.3 12.3 %collective-permute-start.3 = (bf16[256,768]{1,0:T(8,128)(2,1)}, bf16[256,768]{1,0:T(8,128)(2,1)}, u32[]{:S(2)}, u32[]{:S(2)}) collective-permute-start(bf16[256,768]{1,0:T(8,128)(2,1)} %get-tuple-element.26), channel_id=1, source_target_pairs={{0,8},{8,0},{16,24},{24,16},{1,9},{9,1},{17,25},{25,17},{2,10},{10... | collective-permute-start | bytes 1179656 | tf_op jit(solution)/shard_map/ppermute | solution.py:299
  143.8 18.6 %collective-permute-start.2 = (bf16[256,768]{1,0:T(8,128)(2,1)}, bf16[256,768]{1,0:T(8,128)(2,1)}, u32[]{:S(2)}, u32[]{:S(2)}) collective-permute-start(bf16[256,768]{1,0:T(8,128)(2,1)} %get-tuple-element.24), channel_id=1, source_target_pairs={{0,8},{8,0},{16,24},{24,16},{1,9},{9,1},{17,25},{25,17},{2,10},{10... | collective-permute-start | bytes 1179656 | tf_op jit(solution)/shard_map/ppermute | solution.py:299
  163.9 3.7 %collective-permute-start.4 = (f32[512]{0:T(512)S(1)}, f32[512]{0:T(512)S(1)}, u32[]{:S(2)}, u32[]{:S(2)}) collective-permute-start(f32[512]{0:T(512)S(1)} %pad_maximum_fusion.6), channel_id=1, source_target_pairs={{0,8},{8,0},{16,24},{24,16},{1,9},{9,1},{17,25},{25,17},{2,10},{10... | collective-permute-start | bytes 6152 | tf_op jit(solution)/shard_map/ppermute | solution.py:308

commit v4 on v3

--- a/solution.py
+++ b/solution.py
@@ -10,7 +10,7 @@
 DILATION_STEP = 4
 eps_shrink = 0.001
 B = 128
-R = 8
+R = 16
 HIGHEST = lax.Precision.HIGHEST
 NT = (((1,), (1,)), ((), ()))
 NN = (((1,), (0,)), ((), ()))

time: 169 us -> 152 us (0.90)
  Pallas kernels: 90.5 us -> 74.4 us
    pallas_call x1, Pallas kernels: 50.6 us -> 34.5 us  [inverse_factor(): pl.pallas_call(functools.partial(factor_kernel, n), out_shape=jax.ShapeDt...]
  transfers between devices with their start and end apart: 5 -> 5, of which waited for: 3 -> 3; matrix products, arithmetic and copies ran while one was open for 11% -> 12% of each run, Pallas kernels for 0% -> 0%
where the time goes in v4:
time: 152 us
  Pallas kernels  74.4 us (49%)
  matrix products  40.7 us (27%)
  waiting for transfers between devices  13.5 us (9%)
  other arithmetic  8.54 us (6%)
  starting transfers between devices  7.91 us (5%)
  local copies, waits for them, and re-layouts  5.32 us (4%)
  between operations  1.64 us (1%)
    pallas_call x1, Pallas kernels, reduce_and_gather(): pl.pallas_call(functools.partial(reduce_kernel, n, chunks), out_shape=(ja...  40 us
    pallas_call x1, Pallas kernels, inverse_factor(): pl.pallas_call(functools.partial(factor_kernel, n), out_shape=jax.ShapeDt...  34.5 us
    dot_general x12, matrix products, dot(): lax.dot_general(a, b, dims, precision=precision, preferred_element_type=j...  22.1 us
    ppermute x2, waiting for transfers between devices, per_device(): arrived.append(lax.ppermute(first.astype(jnp.bfloat16), 'view', pairs))  11.4 us
    dot_general x2, matrix products, per_device(): jnp.dot(shifted_input, conv_weight[frame_index], preferred_element_type=j...  9.69 us
    dot_general x1, matrix products, per_device(): embed = jnp.dot(hidden, proj_weight, preferred_element_type=jnp.float32)  8.92 us
    unnamed x18, local copies, waits for them, and re-layouts  3.44 us
  transfers between devices with their start and end apart: 5, of which 3 were waited for; matrix products, arithmetic and copies ran while one was open for 12% of the time, Pallas kernels for 0%

profile of v4, /device:TPU:0, one launch (start us, length us, event | category | flops | bytes accessed | tf_op | source)
XLA Modules:
  0.0 152.0 jit_solution(358284632949710680)
XLA Ops:
  1.5 1.3 collective-permute-start.1
  2.8 3.0 %collective-permute-start = (bf16[4,768]{1,0:T(4,128)(2,1)S(1)}, bf16[4,768]{1,0:T(4,128)(2,1)S(1)}, u32[]{:S(2)}, u32[]{:S(2)}) collective-permute-start(bf16[4,768]{1,0:T(4,128)(2,1)S(1)} %get-tuple-element.14), channel_id=1, source_target_pairs={{0,1},{1,2},{2,3},{3,4},{4,5},{5,6},{6,7},{8,9},{9,10},{10,11},{11... | collective-permute-start | bytes 18440 | tf_op jit(solution)/shard_map/ppermute | solution.py:229
  5.9 1.3 convert_reduce_fusion
  7.2 4.8 %fusion.21 = f32[1024,768]{1,0:T(8,128)} fusion(bf16[3,768,768]{2,1,0:T(8,128)(2,1)} %param.7, bf16[1,1024,768]{2,1,0:T(8,128)(2,1)} %param.6), kind=kOutput, calls=%fused_computation.29 | convolution fusion | flops 1207959552 | bytes 5898240 | tf_op jit(solution)/shard_map/dot_general | solution.py:254
  13.3 4.9 %fusion.12 = f32[1024,768]{1,0:T(8,128)} fusion(bf16[1024,768]{1,0:T(8,128)(2,1)} %bitcast.43, bf16[4,768]{1,0:T(4,128)(2,1)S(1)} %collective-permute-done, bf16[3,768,768]{2,1,0:T(8,128)(2,1)} %param.7), kind=kOutput, calls=%fused_computation.16 | convolution fusion | flops 1211105280 | bytes 5904384 | tf_op jit(solution)/shard_map/dot_general | solution.py:254
  18.1 8.9 %fusion.73 = (f32[768]{0:T(1024)S(1)}, f32[1024,768]{1,0:T(8,128)}) fusion(bf16[768,768]{1,0:T(8,128)(2,1)S(1)} %copy-done, f32[1024,768]{1,0:T(8,128)} %fusion.21, f32[1024,768]{1,0:T(8,128)} %fusion.12, bf16[4,768]{1,0:T(4,128)(2,1)S(1)} %collective-permute-done.1, bf16[1024,768]{1,0:T(8,128)(2,1)} %bitcast.44, f32[768]{0:T(1024)S(1)} %copy-done.5, ...), kind=kOutput, calls=%fused_computation.128 | convolution fusion | flops 2432433408 | bytes 13398016 | tf_op jit(solution)/shard_map/dot_general | solution.py:259
  27.7 2.4 %subtract_multiply_fusion = f32[1024,768]{1,0:T(8,128)S(1)} fusion(f32[1024,768]{1,0:T(8,128)} %get-tuple-element.22, f32[768]{0:T(1024)S(1)} %broadcast_divide_fusion.1, f32[1024]{0:T(1024)S(1)} %get-tuple-element.20), kind=kLoop, calls=%fused_computation.10 | loop fusion | flops 1572864 | bytes 6298624 | tf_op jit(solution)/shard_map/mul | solution.py:264
  30.1 1.9 %fusion.31 = f32[256,256]{1,0:T(8,128)S(1)} fusion(f32[1024,768]{1,0:T(8,128)S(1)} %subtract_multiply_fusion), kind=kOutput, calls=%fused_computation.41 | convolution fusion | flops 805306368 | bytes 1310720 | tf_op jit(solution)/shard_map/dot_general | solution.py:21
  32.0 2.1 %fusion.9 = f32[256,512]{1,0:T(8,128)S(1)} fusion(f32[1024,768]{1,0:T(8,128)S(1)} %subtract_multiply_fusion), kind=kOutput, calls=%fused_computation.11 | convolution fusion | flops 1610612736 | bytes 3670016 | tf_op jit(solution)/shard_map/dot_general | solution.py:21
  34.1 3.2 %fusion.28 = f32[256,768]{1,0:T(8,128)S(1)} fusion(f32[1024,768]{1,0:T(8,128)S(1)} %subtract_multiply_fusion), kind=kOutput, calls=%fused_computation.38 | convolution fusion | flops 2415919104 | bytes 4980736 | tf_op jit(solution)/shard_map/dot_general | solution.py:21
  37.5 40.0 %shard_map.77 = (f32[128,2688]{1,0:T(8,128)S(1)}, f32[8,1,896]{2,1,0:T(1,128)S(1)}) custom-call(f32[128,2688]{1,0:T(8,128)S(1)} %slice_dynamic-update-slice_fusion.x_ref, f32[1,896]{1,0:T(1,128)S(1)} %broadcast_in_dim.11.stats_ref), custom_call_target="tpu_custom_call" | custom-call | tf_op jit(solution)/shard_map/pallas_call | solution.py:200
  81.4 0.9 divide_add_fusion.gram_ref
  82.3 34.5 %shard_map.78 = f32[768,768]{1,0:T(8,128)S(1)} custom-call(f32[128,2688]{1,0:T(8,128)S(1)} %divide_add_fusion.gram_ref), custom_call_target="tpu_custom_call" | custom-call | tf_op jit(solution)/shard_map/pallas_call | solution.py:97
  117.0 1.7 %copy-done.1 = f32[1024,768]{1,0:T(8,128)S(1)} copy-done((f32[1024,768]{1,0:T(8,128)S(1)}, f32[1024,768]{1,0:T(8,128)}, u32[]{:S(2)}) %copy-start.1) | copy-done | bytes 3145752
  118.6 3.0 %bitcast_dynamic-update-slice_fusion.2 = (f32[1,1024,768]{2,1,0:T(8,128)S(1)}, bf16[256,768]{1,0:T(8,128)(2,1)}) fusion(f32[1,1024,768]{2,1,0:T(8,128)S(1)} %broadcast_in_dim.10, s32[]{:T(128)S(6)} %select_n.38, f32[768,768]{1,0:T(8,128)S(1)} %shard_map.78, f32[1024,768]{1,0:T(8,128)S(1)} %copy-done.1, f32[768]{0:T(1024)S(1)} %broadcast_divide_fusion, ...), kind=kOutput, calls=%fused_computation.50 | convolution fusion | flops 1812529152 | bytes 4331520 | tf_op jit(solution)/shard_map/dot_general | solution.py:21
  121.6 3.0 %bitcast_dynamic-update-slice_fusion.1 = (f32[1,1024,768]{2,1,0:T(8,128)S(1)}, bf16[256,768]{1,0:T(8,128)(2,1)}) fusion(f32[1,1024,768]{2,1,0:T(8,128)S(1)} %get-tuple-element.23, s32[]{:T(128)S(6)} %select_n.39, f32[768,768]{1,0:T(8,128)S(1)} %shard_map.78, f32[1024,768]{1,0:T(8,128)S(1)} %copy-done.1, f32[256]{0:T(256)S(1)} %get-tuple-element.17, ...), kind=kOutput, calls=%fused_computation.49 | convolution fusion | flops 1812529152 | bytes 4331520 | tf_op jit(solution)/shard_map/dot_general | solution.py:21
  124.5 1.7 %copy-done.2 = f32[1,1024,768]{2,1,0:T(8,128)} copy-done((f32[1,1024,768]{2,1,0:T(8,128)}, f32[1,1024,768]{2,1,0:T(8,128)S(1)}, u32[]{:S(2)}) %copy-start.2) | copy-done | bytes 3145752
  126.2 1.5 collective-permute-start.3
  128.3 6.6 %bitcast_dynamic-update-slice_fusion = (f32[1,1024,768]{2,1,0:T(8,128)}, f32[512,768]{1,0:T(8,128)S(1)}) fusion(f32[1,1024,768]{2,1,0:T(8,128)} %copy-done.2, s32[]{:T(128)S(6)} %select_n.40, f32[768,768]{1,0:T(8,128)S(1)} %shard_map.78, f32[1024,768]{1,0:T(8,128)} %get-tuple-element.22, f32[768]{0:T(1024)S(1)} %broadcast_divide_fusion, ...), kind=kOutput, calls=%fused_computation.18 | convolution fusion | flops 3624665088 | bytes 7084032 | tf_op jit(solution)/shard_map/dot_general | solution.py:21
  134.9 3.5 %collective-permute-done.3 = bf16[256,768]{1,0:T(8,128)(2,1)} collective-permute-done((bf16[256,768]{1,0:T(8,128)(2,1)}, bf16[256,768]{1,0:T(8,128)(2,1)}, u32[]{:S(2)}, u32[]{:S(2)}) %collective-permute-start.3) | collective-permute-done | bytes 393248 | tf_op jit(solution)/shard_map/ppermute | solution.py:299
  138.5 7.9 %collective-permute-done.2 = bf16[256,768]{1,0:T(8,128)(2,1)} collective-permute-done((bf16[256,768]{1,0:T(8,128)(2,1)}, bf16[256,768]{1,0:T(8,128)(2,1)}, u32[]{:S(2)}, u32[]{:S(2)}) %collective-permute-start.2) | collective-permute-done | bytes 393248 | tf_op jit(solution)/shard_map/ppermute | solution.py:299
  146.3 1.4 fusion.36
  147.8 1.6 %collective-permute-start.4 = (f32[512]{0:T(512)S(1)}, f32[512]{0:T(512)S(1)}, u32[]{:S(2)}, u32[]{:S(2)}) collective-permute-start(f32[512]{0:T(512)S(1)} %pad_maximum_fusion.6), channel_id=1, source_target_pairs={{0,8},{8,0},{16,24},{24,16},{1,9},{9,1},{17,25},{25,17},{2,10},{10... | collective-permute-start | bytes 6152 | tf_op jit(solution)/shard_map/ppermute | solution.py:308
  149.3 2.1 %collective-permute-done.4 = f32[512]{0:T(512)S(1)} collective-permute-done((f32[512]{0:T(512)S(1)}, f32[512]{0:T(512)S(1)}, u32[]{:S(2)}, u32[]{:S(2)}) %collective-permute-start.4) | collective-permute-done | bytes 2080 | tf_op jit(solution)/shard_map/ppermute | solution.py:308
  (52 shorter events, 7.4 us)
Async XLA Ops:
  0.6 17.5 %copy-start = (bf16[768,768]{1,0:T(8,128)(2,1)S(1)}, bf16[768,768]{1,0:T(8,128)(2,1)}, u32[]{:S(2)}) copy-start(bf16[768,768]{1,0:T(8,128)(2,1)} %param.9) | copy-start | bytes 3538948
  1.5 16.7 %collective-permute-start.1 = (bf16[4,768]{1,0:T(4,128)(2,1)S(1)}, bf16[4,768]{1,0:T(4,128)(2,1)S(1)}, u32[]{:S(2)}, u32[]{:S(2)}) collective-permute-start(bf16[4,768]{1,0:T(4,128)(2,1)S(1)} %get-tuple-element.13), channel_id=1, source_target_pairs={{1,0},{2,1},{3,2},{4,3},{5,4},{6,5},{7,6},{9,8},{10,9},{11,10},{12... | collective-permute-start | bytes 18440 | tf_op jit(solution)/shard_map/ppermute | solution.py:230
  2.8 10.5 %collective-permute-start = (bf16[4,768]{1,0:T(4,128)(2,1)S(1)}, bf16[4,768]{1,0:T(4,128)(2,1)S(1)}, u32[]{:S(2)}, u32[]{:S(2)}) collective-permute-start(bf16[4,768]{1,0:T(4,128)(2,1)S(1)} %get-tuple-element.14), channel_id=1, source_target_pairs={{0,1},{1,2},{2,3},{3,4},{4,5},{5,6},{6,7},{8,9},{9,10},{10,11},{11... | collective-permute-start | bytes 18440 | tf_op jit(solution)/shard_map/ppermute | solution.py:229
  7.2 4.8 %copy-start.3 = (s32[1024]{0:T(1024)S(1)}, s32[1024]{0:T(1024)}, u32[]{:S(2)}) copy-start(s32[1024]{0:T(1024)} %param.10) | copy-start | bytes 12292
  7.2 4.8 %copy-start.4 = (s32[1024]{0:T(1024)S(1)}, s32[1024]{0:T(1024)}, u32[]{:S(2)}) copy-start(s32[1024]{0:T(1024)} %param.11) | copy-start | bytes 12292
  13.3 4.9 %copy-start.5 = (f32[768]{0:T(1024)S(1)}, f32[768]{0:T(1024)}, u32[]{:S(2)}) copy-start(f32[768]{0:T(1024)} %param.8) | copy-start | bytes 9220
  116.7 1.9 %copy-start.1 = (f32[1024,768]{1,0:T(8,128)S(1)}, f32[1024,768]{1,0:T(8,128)}, u32[]{:S(2)}) copy-start(f32[1024,768]{1,0:T(8,128)} %get-tuple-element.22) | copy-start | bytes 9437188
  124.5 1.7 %copy-start.2 = (f32[1,1024,768]{2,1,0:T(8,128)}, f32[1,1024,768]{2,1,0:T(8,128)S(1)}, u32[]{:S(2)}) copy-start(f32[1,1024,768]{2,1,0:T(8,128)S(1)} %get-tuple-element.25) | copy-start | bytes 9437188
  126.2 12.3 %collective-permute-start.3 = (bf16[256,768]{1,0:T(8,128)(2,1)}, bf16[256,768]{1,0:T(8,128)(2,1)}, u32[]{:S(2)}, u32[]{:S(2)}) collective-permute-start(bf16[256,768]{1,0:T(8,128)(2,1)} %get-tuple-element.26), channel_id=1, source_target_pairs={{0,8},{8,0},{16,24},{24,16},{1,9},{9,1},{17,25},{25,17},{2,10},{10... | collective-permute-start | bytes 1179656 | tf_op jit(solution)/shard_map/ppermute | solution.py:299
  127.7 18.6 %collective-permute-start.2 = (bf16[256,768]{1,0:T(8,128)(2,1)}, bf16[256,768]{1,0:T(8,128)(2,1)}, u32[]{:S(2)}, u32[]{:S(2)}) collective-permute-start(bf16[256,768]{1,0:T(8,128)(2,1)} %get-tuple-element.24), channel_id=1, source_target_pairs={{0,8},{8,0},{16,24},{24,16},{1,9},{9,1},{17,25},{25,17},{2,10},{10... | collective-permute-start | bytes 1179656 | tf_op jit(solution)/shard_map/ppermute | solution.py:299
  147.8 3.7 %collective-permute-start.4 = (f32[512]{0:T(512)S(1)}, f32[512]{0:T(512)S(1)}, u32[]{:S(2)}, u32[]{:S(2)}) collective-permute-start(f32[512]{0:T(512)S(1)} %pad_maximum_fusion.6), channel_id=1, source_target_pairs={{0,8},{8,0},{16,24},{24,16},{1,9},{9,1},{17,25},{25,17},{2,10},{10... | collective-permute-start | bytes 6152 | tf_op jit(solution)/shard_map/ppermute | solution.py:308

commit v5 on v2

--- a/solution.py
+++ b/solution.py
@@ -10,7 +10,7 @@
 DILATION_STEP = 4
 eps_shrink = 0.001
 B = 128
-R = 8
+R = 16
 HIGHEST = lax.Precision.HIGHEST
 NT = (((1,), (1,)), ((), ()))
 NN = (((1,), (0,)), ((), ()))
@@ -281,16 +281,20 @@
     )
     ridge = lower_blocks(lambda i: eps_shrink * jnp.eye(B, (i + 1) * B, i * B, dtype=jnp.float32), n)
     inverse = inverse_factor((gram + between) / count + ridge, width)
-    centered = live[:, None] * (embed - mean[None, :])
-    whitened = dot(centered, inverse, NT)
+
+    def whiten(start, size):
+        rows = lax.dynamic_slice_in_dim(embed, start, size)
+        here = lax.dynamic_slice_in_dim(live, start, size)
+        return dot(here[:, None] * (rows - mean[None, :]), inverse, NT)
 
     half = frame_rows // 2
     bit = lax.axis_index("view") % 2
     pairs = [(i, i ^ 1) for i in range(lax.axis_size("view"))]
-    sent = lax.dynamic_slice_in_dim(whitened, (1 - bit) * half, half).astype(jnp.bfloat16)
-    partner = lax.ppermute(sent, "view", pairs).astype(jnp.float32)
-    own = lax.dynamic_slice_in_dim(whitened, bit * half, half)
-    diff = own - partner
+    first = whiten((1 - bit) * half, half)
+    arrived = lax.ppermute(first.astype(jnp.bfloat16), "view", pairs)
+    own = whiten(bit * half, half)
+    whitened = jnp.where(bit == 0, jnp.concatenate([own, first]), jnp.concatenate([first, own]))
+    diff = own - arrived.astype(jnp.float32)
     mine = jnp.sum(diff * diff, axis=1) / width
     theirs = lax.ppermute(mine, "view", pairs)
     pair_loss = jnp.where(bit == 0, jnp.concatenate([mine, theirs]), jnp.concatenate([theirs, mine]))

time: 170 us -> 153 us (0.900)
  Pallas kernels: 91.3 us -> 75.2 us
  local copies, waits for them, and re-layouts: 6.94 us -> 1.71 us
  matrix products: 36.4 us -> 39.6 us
    pallas_call x1, Pallas kernels: 50.6 us -> 34.5 us  [inverse_factor(): pl.pallas_call(functools.partial(factor_kernel, n), out_shape=jax.ShapeDt...]
    unnamed x19 -> x18, local copies, waits for them, and re-layouts: 5.31 us -> 0.12 us
    dot_general x10 -> x11, matrix products: 17.8 us -> 21 us  [dot(): lax.dot_general(a, b, dims, precision=precision, preferred_element_type=j...]
    select_n x0 -> x1, other arithmetic: none -> 1.93 us  [per_device(): jnp.where(bit == 0, jnp.concatenate([own, first]), jnp.concatenate([first...]
  transfers between devices with their start and end apart: 4 -> 4, of which waited for: 1 -> 2; matrix products, arithmetic and copies ran while one was open for 9% -> 9% of each run, Pallas kernels for 0% -> 0%
where the time goes in v5:
time: 153 us
  Pallas kernels  75.2 us (49%)
  matrix products  39.6 us (26%)
  waiting for transfers between devices  18.8 us (12%)
  other arithmetic  9.05 us (6%)
  starting transfers between devices  6.69 us (4%)
  local copies, waits for them, and re-layouts  1.71 us (1%)
  between operations  1.64 us (1%)
    pallas_call x1, Pallas kernels, reduce_and_gather(): pl.pallas_call(functools.partial(reduce_kernel, n, chunks), out_shape=(ja...  40.7 us
    pallas_call x1, Pallas kernels, inverse_factor(): pl.pallas_call(functools.partial(factor_kernel, n), out_shape=jax.ShapeDt...  34.5 us
    dot_general x11, matrix products, dot(): lax.dot_general(a, b, dims, precision=precision, preferred_element_type=j...  21 us
    ppermute x1, waiting for transfers between devices, per_device(): arrived = lax.ppermute(first.astype(jnp.bfloat16), 'view', pairs)  18.6 us
    dot_general x2, matrix products, per_device(): jnp.dot(shifted_input, conv_weight[frame_index], preferred_element_type=j...  9.69 us
    dot_general x1, matrix products, per_device(): embed = jnp.dot(hidden, proj_weight, preferred_element_type=jnp.float32)  8.92 us
  transfers between devices with their start and end apart: 4, of which 2 were waited for; matrix products, arithmetic and copies ran while one was open for 9% of the time, Pallas kernels for 0%

profile of v5, /device:TPU:0, one launch (start us, length us, event | category | flops | bytes accessed | tf_op | source)
XLA Modules:
  0.0 152.7 jit_solution(14078386120792486804)
XLA Ops:
  0.6 0.8 slice_bitcast_fusion
  1.5 2.4 %collective-permute-start = (bf16[4,768]{1,0:T(4,128)(2,1)S(1)}, bf16[4,768]{1,0:T(4,128)(2,1)S(1)}, u32[]{:S(2)}, u32[]{:S(2)}) collective-permute-start(bf16[4,768]{1,0:T(4,128)(2,1)S(1)} %get-tuple-element.12), channel_id=1, source_target_pairs={{0,1},{1,2},{2,3},{3,4},{4,5},{5,6},{6,7},{8,9},{9,10},{10,11},{11... | collective-permute-start | bytes 18440 | tf_op jit(solution)/shard_map/ppermute | solution.py:229
  3.8 1.3 collective-permute-start.1
  5.2 1.3 convert_reduce_fusion
  6.5 4.8 %fusion.25 = f32[1024,768]{1,0:T(8,128)} fusion(bf16[3,768,768]{2,1,0:T(8,128)(2,1)} %param.7, bf16[1,1024,768]{2,1,0:T(8,128)(2,1)} %param.6), kind=kOutput, calls=%fused_computation.34 | convolution fusion | flops 1207959552 | bytes 5898240 | tf_op jit(solution)/shard_map/dot_general | solution.py:254
  12.6 4.9 %fusion.12 = f32[1024,768]{1,0:T(8,128)} fusion(bf16[1024,768]{1,0:T(8,128)(2,1)} %bitcast.38, bf16[4,768]{1,0:T(4,128)(2,1)S(1)} %collective-permute-done, bf16[3,768,768]{2,1,0:T(8,128)(2,1)} %param.7), kind=kOutput, calls=%fused_computation.17 | convolution fusion | flops 1211105280 | bytes 5904384 | tf_op jit(solution)/shard_map/dot_general | solution.py:254
  17.5 8.9 %fusion.62 = (f32[768]{0:T(1024)S(1)}, f32[1024,768]{1,0:T(8,128)}) fusion(bf16[768,768]{1,0:T(8,128)(2,1)S(1)} %copy-done, f32[1024,768]{1,0:T(8,128)} %fusion.25, f32[1024,768]{1,0:T(8,128)} %fusion.12, bf16[4,768]{1,0:T(4,128)(2,1)S(1)} %collective-permute-done.1, bf16[1024,768]{1,0:T(8,128)(2,1)} %bitcast.39, f32[768]{0:T(1024)S(1)} %copy-done.5, ...), kind=kOutput, calls=%fused_computation.112 | convolution fusion | flops 2432433408 | bytes 13398016 | tf_op jit(solution)/shard_map/dot_general | solution.py:259
  26.4 2.4 %subtract_multiply_fusion = f32[1024,768]{1,0:T(8,128)S(1)} fusion(f32[1024,768]{1,0:T(8,128)} %get-tuple-element.20, f32[768]{0:T(1024)S(1)} %broadcast_divide_fusion.1, f32[1024]{0:T(1024)S(1)} %get-tuple-element.18), kind=kLoop, calls=%fused_computation.11 | loop fusion | flops 1572864 | bytes 6298624 | tf_op jit(solution)/shard_map/mul | solution.py:264
  28.8 1.9 %fusion.35 = f32[256,256]{1,0:T(8,128)S(1)} fusion(f32[1024,768]{1,0:T(8,128)S(1)} %subtract_multiply_fusion), kind=kOutput, calls=%fused_computation.46 | convolution fusion | flops 805306368 | bytes 1310720 | tf_op jit(solution)/shard_map/dot_general | solution.py:21
  30.7 2.1 %fusion.9 = f32[256,512]{1,0:T(8,128)S(1)} fusion(f32[1024,768]{1,0:T(8,128)S(1)} %subtract_multiply_fusion), kind=kOutput, calls=%fused_computation.12 | convolution fusion | flops 1610612736 | bytes 3670016 | tf_op jit(solution)/shard_map/dot_general | solution.py:21
  32.8 3.2 %fusion.32 = f32[256,768]{1,0:T(8,128)S(1)} fusion(f32[1024,768]{1,0:T(8,128)S(1)} %subtract_multiply_fusion), kind=kOutput, calls=%fused_computation.43 | convolution fusion | flops 2415919104 | bytes 4980736 | tf_op jit(solution)/shard_map/dot_general | solution.py:21
  36.0 0.7 concatenate.70
  36.9 40.7 %shard_map.77 = (f32[128,2688]{1,0:T(8,128)S(1)}, f32[8,1,896]{2,1,0:T(1,128)S(1)}) custom-call(f32[128,2688]{1,0:T(8,128)S(1)} %slice_dynamic-update-slice_fusion.x_ref, f32[1,896]{1,0:T(1,128)S(1)} %broadcast_in_dim.2.stats_ref), custom_call_target="tpu_custom_call" | custom-call | tf_op jit(solution)/shard_map/pallas_call | solution.py:200
  77.6 0.6 sqrt_reduce_fusion
  78.3 0.7 broadcast_divide_fusion
  81.4 0.9 divide_add_fusion.gram_ref
  82.4 34.5 %shard_map.78 = f32[768,768]{1,0:T(8,128)S(1)} custom-call(f32[128,2688]{1,0:T(8,128)S(1)} %divide_add_fusion.gram_ref), custom_call_target="tpu_custom_call" | custom-call | tf_op jit(solution)/shard_map/pallas_call | solution.py:97
  116.8 5.5 %fusion.65 = (bf16[512,768]{1,0:T(8,128)(2,1)}, f32[512,768]{1,0:T(8,128)}) fusion(f32[768,768]{1,0:T(8,128)S(1)} %shard_map.78, f32[1024,768]{1,0:T(8,128)S(1)} %copy-done.1, s32[]{:T(128)S(6)} %select_n.48, f32[512]{0:T(512)S(1)} %get-tuple-element.16, f32[768]{0:T(1024)S(1)} %broadcast_divide_fusion), kind=kOutput, calls=%fused_computation.113 | convolution fusion | flops 3625058304 | bytes 6297604 | tf_op jit(solution)/shard_map/dot_general | solution.py:21
  122.3 1.5 collective-permute-start.2
  123.8 18.6 %collective-permute-done.2 = bf16[512,768]{1,0:T(8,128)(2,1)} collective-permute-done((bf16[512,768]{1,0:T(8,128)(2,1)}, bf16[512,768]{1,0:T(8,128)(2,1)}, u32[]{:S(2)}, u32[]{:S(2)}) %collective-permute-start.2) | collective-permute-done | bytes 786464 | tf_op jit(solution)/shard_map/ppermute | solution.py:294
  142.4 6.0 %multiply_reduce_fusion = (f32[512]{0:T(512)S(1)}, f32[512,768]{1,0:T(8,128)S(1)}) fusion(bf16[512,768]{1,0:T(8,128)(2,1)} %collective-permute-done.2, f32[768,768]{1,0:T(8,128)S(1)} %shard_map.78, f32[1024,768]{1,0:T(8,128)} %get-tuple-element.20, s32[]{:T(128)S(6)} %select_n.47, f32[768]{0:T(1024)S(1)} %broadcast_divide_fusion, f32[512]{0:T(512)S(1)} %get-tuple-element.15), kind=kOutput, calls=%fused_computation.19 | convolution fusion | flops 3626237440 | bytes 6298628 | tf_op jit(solution)/shard_map/dot_general | solution.py:21
  148.4 1.5 %collective-permute-start.3 = (f32[512]{0:T(512)S(1)}, f32[512]{0:T(512)S(1)}, u32[]{:S(2)}, u32[]{:S(2)}) collective-permute-start(f32[512]{0:T(512)S(1)} %broadcast_multiply_fusion), channel_id=1, source_target_pairs={{0,8},{8,0},{16,24},{24,16},{1,9},{9,1},{17,25},{25,17},{2,10},{10... | collective-permute-start | bytes 6152 | tf_op jit(solution)/shard_map/ppermute | solution.py:299
  150.0 1.9 %maximum_select_fusion = f32[1,1024,768]{2,1,0:T(8,128)} fusion(f32[1,512,768]{2,1,0:T(8,128)S(1)} %bitcast.31, f32[1,512,768]{2,1,0:T(8,128)S(1)} %bitcast.32, pred[]{:T(512)S(6)} %eq.24), kind=kLoop, calls=%fused_computation.10 | loop fusion | flops 2359296 | bytes 6291457 | tf_op jit(solution)/shard_map/jit(_where)/select_n | solution.py:296
  152.1 0.6 broadcast_select_fusion
  (46 shorter events, 3.4 us)
Async XLA Ops:
  0.6 16.8 %copy-start = (bf16[768,768]{1,0:T(8,128)(2,1)S(1)}, bf16[768,768]{1,0:T(8,128)(2,1)}, u32[]{:S(2)}) copy-start(bf16[768,768]{1,0:T(8,128)(2,1)} %param.9) | copy-start | bytes 3538948
  1.5 11.1 %collective-permute-start = (bf16[4,768]{1,0:T(4,128)(2,1)S(1)}, bf16[4,768]{1,0:T(4,128)(2,1)S(1)}, u32[]{:S(2)}, u32[]{:S(2)}) collective-permute-start(bf16[4,768]{1,0:T(4,128)(2,1)S(1)} %get-tuple-element.12), channel_id=1, source_target_pairs={{0,1},{1,2},{2,3},{3,4},{4,5},{5,6},{6,7},{8,9},{9,10},{10,11},{11... | collective-permute-start | bytes 18440 | tf_op jit(solution)/shard_map/ppermute | solution.py:229
  3.8 13.6 %collective-permute-start.1 = (bf16[4,768]{1,0:T(4,128)(2,1)S(1)}, bf16[4,768]{1,0:T(4,128)(2,1)S(1)}, u32[]{:S(2)}, u32[]{:S(2)}) collective-permute-start(bf16[4,768]{1,0:T(4,128)(2,1)S(1)} %get-tuple-element.11), channel_id=1, source_target_pairs={{1,0},{2,1},{3,2},{4,3},{5,4},{6,5},{7,6},{9,8},{10,9},{11,10},{12... | collective-permute-start | bytes 18440 | tf_op jit(solution)/shard_map/ppermute | solution.py:230
  6.5 4.8 %copy-start.3 = (s32[1024]{0:T(1024)S(1)}, s32[1024]{0:T(1024)}, u32[]{:S(2)}) copy-start(s32[1024]{0:T(1024)} %param.10) | copy-start | bytes 12292
  6.5 4.8 %copy-start.4 = (s32[1024]{0:T(1024)S(1)}, s32[1024]{0:T(1024)}, u32[]{:S(2)}) copy-start(s32[1024]{0:T(1024)} %param.11) | copy-start | bytes 12292
  12.6 4.9 %copy-start.5 = (f32[768]{0:T(1024)S(1)}, f32[768]{0:T(1024)}, u32[]{:S(2)}) copy-start(f32[768]{0:T(1024)} %param.8) | copy-start | bytes 9220
  82.4 34.5 %copy-start.1 = (f32[1024,768]{1,0:T(8,128)S(1)}, f32[1024,768]{1,0:T(8,128)}, u32[]{:S(2)}) copy-start(f32[1024,768]{1,0:T(8,128)} %get-tuple-element.20) | copy-start | bytes 9437188
  122.3 20.1 %collective-permute-start.2 = (bf16[512,768]{1,0:T(8,128)(2,1)}, bf16[512,768]{1,0:T(8,128)(2,1)}, u32[]{:S(2)}, u32[]{:S(2)}) collective-permute-start(bf16[512,768]{1,0:T(8,128)(2,1)} %get-tuple-element.21), channel_id=1, source_target_pairs={{0,8},{8,0},{16,24},{24,16},{1,9},{9,1},{17,25},{25,17},{2,10},{10... | collective-permute-start | bytes 2359304 | tf_op jit(solution)/shard_map/ppermute | solution.py:294
  142.4 7.5 %copy-start.2 = (f32[512,768]{1,0:T(8,128)S(1)}, f32[512,768]{1,0:T(8,128)}, u32[]{:S(2)}) copy-start(f32[512,768]{1,0:T(8,128)} %get-tuple-element.22) | copy-start | bytes 4718596
  148.4 3.7 %collective-permute-start.3 = (f32[512]{0:T(512)S(1)}, f32[512]{0:T(512)S(1)}, u32[]{:S(2)}, u32[]{:S(2)}) collective-permute-start(f32[512]{0:T(512)S(1)} %broadcast_multiply_fusion), channel_id=1, source_target_pairs={{0,8},{8,0},{16,24},{24,16},{1,9},{9,1},{17,25},{25,17},{2,10},{10... | collective-permute-start | bytes 6152 | tf_op jit(solution)/shard_map/ppermute | solution.py:299
